TPU v7x, 256 devices: a whole 4x4x8 slice. The times are simulated.
256 devices in a mesh: ja: 16 (over y_hi, z), ka: 16 (over x, y_lo, core).
Axes of the slice: x: 4, y: 4 (y_hi: 2, y_lo: 2; y = y_hi * 2 + y_lo), z: 8, core: 2. Of those that a mesh axis runs over, the one named last changes fastest.
Arguments:
- pair_map: float32 [1536, 1536, 128], P('ja', 'ka'), may hold values from -45 to 45
- slab_rows: float32 [128, 1536, 128], P('ja', 'ka'), may hold values from -45 to 45
- norm_gain: float32 [128], replicated, may hold values from 0.1 to 1.9
- left_gate: float32 [128, 128], replicated, may hold values from -0.5 to 0.5
- left_value: float32 [128, 128], replicated, may hold values from -0.5 to 0.5
- right_gate: float32 [128, 128], replicated, may hold values from -0.5 to 0.5
- right_value: float32 [128, 128], replicated, may hold values from -0.5 to 0.5
- out_gain: float32 [128], replicated, may hold values from 0.1 to 1.9
- out_weight: float32 [128, 128], replicated, may hold values from -0.5 to 0.5
- cotangent: float32 [128, 1536, 128], P('ka', 'ja'), may hold values from -6 to 6
Outputs:
- update: float32 [128, 1536, 128], P('ka', 'ja')
- grad_pair: float32 [1536, 1536, 128], P('ja', 'ka')
- grad_slab: float32 [128, 1536, 128], P('ja', 'ka')
All inputs are finite; a program needn't handle non-finite values.
Results may differ from a plain program's by a relative error of at most 0.0003.
Values sent between devices are 32-bit elements; how exact they have to be, the bound alone decides.
A program may use at most 192 MiB of HBM per device.

v0:
```python
import jax
import jax.numpy as jnp
from jax import lax
from jax.sharding import PartitionSpec as P

norm_eps = 1e-05


def layer_norm(values, gain):
    center = values - jnp.mean(values, axis=-1, keepdims=True)
    spread = jnp.mean(center * center, axis=-1, keepdims=True)
    return center * lax.rsqrt(spread + norm_eps) * gain


def project(values, gain, w_gate, w_value):
    normed = layer_norm(values, gain)
    gate = jnp.dot(
        normed, w_gate, precision=lax.Precision.HIGHEST, preferred_element_type=jnp.float32
    )
    value = jnp.dot(
        normed, w_value, precision=lax.Precision.HIGHEST, preferred_element_type=jnp.float32
    )
    return jax.nn.sigmoid(gate) * value


def finish(product, out_gain, out_weight):
    normed = layer_norm(product, out_gain)
    return jnp.dot(
        normed, out_weight, precision=lax.Precision.HIGHEST, preferred_element_type=jnp.float32
    )


def shards(
    pair_map,
    slab_rows,
    norm_gain,
    left_gate,
    left_value,
    right_gate,
    right_value,
    out_gain,
    out_weight,
    cotangent,
):
    right_map, back_right = jax.vjp(
        lambda block: project(block, norm_gain, right_gate, right_value), pair_map
    )
    left_local, back_left = jax.vjp(
        lambda slab: project(slab, norm_gain, left_gate, left_value), slab_rows
    )
    whole_left = lax.all_gather(left_local, "ja", axis=0, tiled=True)

    def finish_rows(prod_in):
        return finish(prod_in, out_gain, out_weight)

    picked = whole_left
    own_sums = lax.psum_scatter(
        jnp.einsum("ikh,jkh->ijh", picked, right_map, precision=lax.Precision.HIGHEST),
        "ka",
        scatter_dimension=0,
        tiled=True,
    )
    update, back_out = jax.vjp(finish_rows, own_sums)
    own_grad = back_out(cotangent)[0]
    grad_product = lax.all_gather(own_grad, "ka", axis=0, tiled=True)
    grad_right = jnp.einsum(
        "ijh,ikh->jkh", grad_product, whole_left, precision=lax.Precision.HIGHEST
    )
    picked = grad_product
    grad_left = lax.psum_scatter(
        jnp.einsum("ijh,jkh->ikh", picked, right_map, precision=lax.Precision.HIGHEST),
        "ja",
        scatter_dimension=0,
        tiled=True,
    )
    grad_slab = back_left(grad_left)[0]
    grad_pair = back_right(grad_right)[0]
    return (update, grad_pair, grad_slab)


def solution(mesh):
    in_specs = (
        P("ja", "ka", None),
        P("ja", "ka", None),
        P(),
        P(),
        P(),
        P(),
        P(),
        P(),
        P(),
        P("ka", "ja", None),
    )
    out_specs = (P("ka", "ja", None), P("ja", "ka", None), P("ja", "ka", None))
    return jax.shard_map(shards, mesh=mesh, in_specs=in_specs, out_specs=out_specs, check_vma=False)
```

profile of v0, /device:TPU:2, one launch (start us, length us, event | category | flops | bytes accessed | tf_op | source)
XLA Modules:
  0.0 569.4 jit_solution(7713918853356801466)
XLA Ops:
  7.2 1.2 reduce_sum.107
  8.5 1.3 multiply_reduce_fusion.5
  9.9 1.6 fusion.30
  11.5 2.4 fusion.62
  14.0 4.0 reduce_sum.105
  18.0 5.7 %multiply_reduce_fusion.1 = f32[96,96]{1,0:T(8,128)S(1)} fusion(f32[96,96,128]{2,1,0:T(8,128)} %param.10, f32[96,96]{1,0:T(8,128)S(1)} %broadcast_multiply_fusion), kind=kLoop, calls=%fused_computation.11 | loop fusion | flops 3529728 | bytes 4792320 | tf_op jit(solution)/shard_map/jvp()/reduce_sum | solution.py:11
  23.8 8.6 %fusion.4 = f32[96,96,128]{2,1,0:T(8,128)S(1)} fusion(f32[96,96,128]{2,1,0:T(8,128)} %param.10, f32[128]{0:T(128)S(1)} %copy-done.11, f32[96,96]{1,0:T(8,128)S(1)} %fusion.56, f32[96,96]{1,0:T(8,128)S(1)} %broadcast_multiply_fusion, f32[128,128]{1,0:T(8,128)S(1)} %copy-done.6), kind=kOutput, calls=%fused_computation.12 | convolution fusion | flops 1815478272 | bytes 9576960 | tf_op jit(solution)/shard_map/jvp()/dot_general | solution.py:20
  32.5 8.8 %fusion.61 = (f32[96,96,128]{2,1,0:T(8,128)}, f32[96,96,128]{2,1,0:T(8,128)}) fusion(f32[96,96,128]{2,1,0:T(8,128)S(1)} %fusion.4, f32[128,128]{1,0:T(8,128)S(1)} %copy-done.9, f32[96,96,128]{2,1,0:T(8,128)S(1)} %bitcast.57, f32[128]{0:T(128)S(1)} %copy-done.11, f32[96,96]{1,0:T(8,128)S(1)} %fusion.56, f32[96,96]{1,0:T(8,128)S(1)} %broadcast_multiply_fusion), kind=kOutput, calls=%fused_computation.93 | convolution fusion | flops 1820196864 | bytes 19014144 | tf_op jit(solution)/shard_map/jvp()/dot_general | solution.py:17
  41.3 6.3 %copy.33 = f32[96,96,128]{0,1,2:T(8,128)} copy(f32[96,96,128]{2,1,0:T(8,128)} %get-tuple-element.7) | data formatting | bytes 9437184 | tf_op jit(solution)/shard_map/jvp()/mul | solution.py:23
  47.6 85.2 %all-gather.3.cloned.1.call-done = f32[128,96,128]{2,1,0:T(8,128)} async-done(((f32[8,96,128]{2,1,0:T(8,128)}), f32[128,96,128]{2,1,0:T(8,128)}) %all-gather.3.cloned.1.call-update) | async-done | bytes 6291472 | tf_op jit(solution)/shard_map/all_gather | solution.py:51
  132.8 8.4 %copy.28 = f32[128,96,128]{1,0,2:T(8,128)} copy(f32[128,96,128]{2,1,0:T(8,128)} %all-gather.3.cloned.1.call-done) | data formatting | bytes 12582912 | tf_op jit(solution)/shard_map/all_gather | solution.py:51
  141.2 22.5 %convolution_bitcast_fusion = f32[128,96,128]{0,1,2:T(8,128)} fusion(f32[96,96,128]{0,1,2:T(8,128)} %copy.33, f32[128,96,128]{1,0,2:T(8,128)} %copy.28), kind=kOutput, calls=%fused_computation.16 | convolution fusion | flops 1811939328 | bytes 17301504 | tf_op jit(solution)/shard_map/ikh,jkh->ijh/dot_general | solution.py:58
  163.7 6.7 %copy.29 = f32[128,96,128]{2,1,0:T(8,128)} copy(f32[128,96,128]{0,1,2:T(8,128)} %convolution_bitcast_fusion) | data formatting | bytes 12582912 | tf_op jit(solution)/shard_map/ikh,jkh->ijh/transpose | solution.py:58
  170.6 73.3 %reduce-scatter.3.cloned.1.call-done = f32[8,96,128]{2,1,0:T(8,128)} async-done(((f32[128,96,128]{2,1,0:T(8,128)}), f32[8,96,128]{2,1,0:T(8,128)}) %reduce-scatter.3.cloned.1.call-update) | async-done | bytes 393232 | tf_op jit(solution)/shard_map/reduce_scatter | solution.py:57
  245.2 1.6 multiply_reduce_fusion.3
  246.9 1.5 fusion.44
  248.4 2.2 broadcast_add_fusion.2
  250.7 48.2 %all-gather.5.cloned.1.call-done = f32[128,96,128]{2,1,0:T(8,128)} async-done(((f32[8,96,128]{2,1,0:T(8,128)}), f32[128,96,128]{2,1,0:T(8,128)}) %all-gather.5.cloned.1.call-update) | async-done | bytes 6291472 | tf_op jit(solution)/shard_map/all_gather | solution.py:65
  298.9 8.4 %copy.31 = f32[128,96,128]{1,0,2:T(8,128)} copy(f32[128,96,128]{2,1,0:T(8,128)} %all-gather.5.cloned.1.call-done) | data formatting | bytes 12582912 | tf_op jit(solution)/shard_map/all_gather | solution.py:65
  307.3 22.2 %fusion.64 = f32[128,96,128]{2,1,0:T(8,128)} fusion(f32[96,96,128]{0,1,2:T(8,128)} %copy.33, f32[128,96,128]{1,0,2:T(8,128)} %copy.31), kind=kOutput, calls=%fused_computation.96 | convolution fusion | flops 1811939328 | bytes 17301504 | tf_op jit(solution)/shard_map/ijh,jkh->ikh/dot_general | solution.py:71
  329.4 6.7 %copy.35 = f32[128,96,128]{0,1,2:T(8,128)} copy(f32[128,96,128]{2,1,0:T(8,128)} %fusion.64) | data formatting | bytes 12582912 | tf_op jit(solution)/shard_map/ijh,jkh->ikh/dot_general | solution.py:71
  337.1 1.3 fusion.27
  338.4 18.8 %fusion.63 = f32[128,96,96]{2,1,0:T(8,128)} fusion(f32[128,96,128]{1,0,2:T(8,128)} %copy.28, f32[128,96,128]{1,0,2:T(8,128)} %copy.31), kind=kOutput, calls=%fused_computation.95 | convolution fusion | flops 1811939328 | bytes 17301504 | tf_op jit(solution)/shard_map/ijh,ikh->jkh/dot_general | solution.py:66
  357.3 6.3 %copy.32 = f32[128,96,96]{0,1,2:T(8,128)} copy(f32[128,96,96]{2,1,0:T(8,128)} %fusion.63) | data formatting | bytes 9437184 | tf_op jit(solution)/shard_map/ijh,ikh->jkh/dot_general | solution.py:66
  363.5 8.1 %fusion.3 = f32[96,96,128]{2,1,0:T(8,128)} fusion(f32[96,96,128]{2,1,0:T(8,128)} %get-tuple-element.8, f32[128,96,96]{0,1,2:T(8,128)} %copy.32, f32[128,128]{1,0:T(8,128)S(1)} %copy-done.6), kind=kOutput, calls=%fused_computation.6 | convolution fusion | flops 1813118976 | bytes 14221312 | tf_op jit(solution)/shard_map/transpose(jvp())/dot_general | solution.py:20
  371.7 8.9 %multiply_reduce_fusion = (f32[96,96]{1,0:T(8,128)S(1)}, f32[96,96,128]{2,1,0:T(8,128)S(1)}) fusion(f32[96,96,128]{2,1,0:T(8,128)S(1)} %bitcast.59, f32[96,96]{1,0:T(8,128)S(1)} %broadcast_multiply_fusion, f32[128]{0:T(128)S(1)} %copy-done.11, f32[96,96,128]{2,1,0:T(8,128)} %fusion.3, f32[128,128]{1,0:T(8,128)S(1)} %copy-done.9, ...), kind=kOutput, calls=%fused_computation.7 | convolution fusion | flops 1822546944 | bytes 28451328 | tf_op jit(solution)/shard_map/transpose(jvp())/dot_general | solution.py:17
  380.7 6.3 %fusion.21 = f32[96,96]{1,0:T(8,128)S(1)} fusion(f32[96,96]{1,0:T(8,128)S(1)} %multiply_multiply_fusion.8, f32[96,96,128]{2,1,0:T(8,128)S(1)} %bitcast.59, f32[96,96]{1,0:T(8,128)S(1)} %broadcast_multiply_fusion, f32[96,96,128]{2,1,0:T(8,128)S(1)} %get-tuple-element.13, f32[96,96]{1,0:T(8,128)S(1)} %fusion.56), kind=kLoop, calls=%fused_computation.32 | loop fusion | flops 7068672 | bytes 9584640 | tf_op jit(solution)/shard_map/transpose(jvp())/reduce_sum | solution.py:10
  387.0 6.6 %broadcast_add_fusion = f32[96,96,128]{2,1,0:T(8,128)} fusion(f32[96,96]{1,0:T(8,128)S(1)} %negate_multiply_fusion, f32[96,96]{1,0:T(8,128)S(1)} %multiply_multiply_fusion.8, f32[96,96,128]{2,1,0:T(8,128)S(1)} %bitcast.59, f32[96,96]{1,0:T(8,128)S(1)} %broadcast_multiply_fusion, f32[96,96,128]{2,1,0:T(8,128)S(1)} %get-tuple-element.13, f32[96,96]{1,0:T(8,128)S(1)} %fusion.56), kind=kLoop, calls=%fused_computation.17 | loop fusion | flops 7077888 | bytes 14303232 | tf_op jit(solution)/shard_map/transpose(jvp())/add_any | solution.py:10
  393.7 164.0 %reduce-scatter.5.cloned.1.call-done = f32[8,96,128]{2,1,0:T(8,128)} async-done(((f32[128,96,128]{2,1,0:T(8,128)}), f32[8,96,128]{2,1,0:T(8,128)}) %reduce-scatter.5.cloned.1.call-update) | async-done | bytes 393232 | tf_op jit(solution)/shard_map/reduce_scatter | solution.py:70
  557.7 1.5 fusion.25
  559.2 1.6 multiply_reduce_fusion.2
  561.4 1.2 broadcast_add_fusion.1
  (57 shorter events, 3.3 us)
Async XLA Ops:
  7.2 238.0 %copy-start = (f32[8,96,128]{2,1,0:T(8,128)S(1)}, f32[8,96,128]{2,1,0:T(8,128)}, u32[]{:S(2)}) copy-start(f32[8,96,128]{2,1,0:T(8,128)} %param.19) | copy-start | bytes 1179652
  7.2 125.6 %all-gather.3.cloned.1.call-start = ((), (), s32[]{:S(2)}) async-start(), calls=%async_computation.2 | async-start | bytes 6684672 | tf_op jit(solution)/shard_map/all_gather | solution.py:51
  13.9 9.9 %copy-start.6 = (f32[128,128]{1,0:T(8,128)S(1)}, f32[128,128]{1,0:T(8,128)}, u32[]{:S(2)}) copy-start(f32[128,128]{1,0:T(8,128)} %param.16) | copy-start | bytes 196612
  13.9 9.9 %copy-start.11 = (f32[128]{0:T(128)S(1)}, f32[128]{0:T(128)}, u32[]{:S(2)}) copy-start(f32[128]{0:T(128)} %param.12) | copy-start | bytes 1540
  13.9 230.0 %reduce-scatter.3.cloned.1.call-start = ((), (), s32[]{:S(2)}) async-start(), calls=%async_computation.3 | async-start | bytes 6684672 | tf_op jit(solution)/shard_map/reduce_scatter | solution.py:57
  18.0 14.4 %slice-start = ((s8[4718592]{0:T(1024)(128)(4,1)}), s8[4194304]{0:T(1024)(128)(4,1)S(1)}, s32[]{:S(2)}) async-start(s8[4718592]{0:T(1024)(128)(4,1)} %bitcast.56), calls=%async_computation.6 | async-start | bytes 8388608
  23.8 8.7 %slice-start.1 = ((s8[4718592]{0:T(1024)(128)(4,1)}), s8[524288]{0:T(1024)(128)(4,1)S(1)}, s32[]{:S(2)}) async-start(s8[4718592]{0:T(1024)(128)(4,1)} %bitcast.56), calls=%async_computation.7 | async-start | bytes 1048576
  23.8 8.7 %copy-start.9 = (f32[128,128]{1,0:T(8,128)S(1)}, f32[128,128]{1,0:T(8,128)}, u32[]{:S(2)}) copy-start(f32[128,128]{1,0:T(8,128)} %param.15) | copy-start | bytes 196612
  32.5 8.8 %copy-start.3 = (f32[96,96,128]{2,1,0:T(8,128)}, f32[96,96,128]{2,1,0:T(8,128)S(1)}, u32[]{:S(2)}) copy-start(f32[96,96,128]{2,1,0:T(8,128)S(1)} %fusion.4) | copy-start | bytes 14155780
  170.4 74.8 %copy-start.7 = (f32[128,128]{1,0:T(8,128)S(1)}, f32[128,128]{1,0:T(8,128)}, u32[]{:S(2)}) copy-start(f32[128,128]{1,0:T(8,128)} %param.18) | copy-start | bytes 196612
  170.4 74.8 %copy-start.12 = (f32[128]{0:T(128)S(1)}, f32[128]{0:T(128)}, u32[]{:S(2)}) copy-start(f32[128]{0:T(128)} %param.17) | copy-start | bytes 1540
  170.4 128.5 %all-gather.5.cloned.1.call-start = ((), (), s32[]{:S(2)}) async-start(), calls=%async_computation.4 | async-start | bytes 6684672 | tf_op jit(solution)/shard_map/all_gather | solution.py:65
  250.7 307.0 %reduce-scatter.5.cloned.1.call-start = ((), (), s32[]{:S(2)}) async-start(), calls=%async_computation.5 | async-start | bytes 6684672 | tf_op jit(solution)/shard_map/reduce_scatter | solution.py:70
  336.1 1.0 copy-start.5
  357.3 14.4 %slice-start.2 = ((s8[4718592]{0:T(1024)(128)(4,1)}), s8[524288]{0:T(1024)(128)(4,1)S(1)}, s32[]{:S(2)}) async-start(s8[4718592]{0:T(1024)(128)(4,1)} %bitcast.58), calls=%async_computation.8 | async-start | bytes 1048576
  363.5 8.1 %slice-start.3 = ((s8[4718592]{0:T(1024)(128)(4,1)}), s8[4194304]{0:T(1024)(128)(4,1)S(1)}, s32[]{:S(2)}) async-start(s8[4718592]{0:T(1024)(128)(4,1)} %bitcast.58), calls=%async_computation.9 | async-start | bytes 8388608
  363.5 8.1 %copy-start.2 = (f32[128,96,96]{0,1,2:T(8,128)S(1)}, f32[128,96,96]{0,1,2:T(8,128)}, u32[]{:S(2)}) copy-start(f32[128,96,96]{0,1,2:T(8,128)} %copy.32) | copy-start | bytes 14155780
  387.0 170.7 %copy-start.8 = (f32[128,128]{1,0:T(8,128)S(1)}, f32[128,128]{1,0:T(8,128)}, u32[]{:S(2)}) copy-start(f32[128,128]{1,0:T(8,128)} %param.14) | copy-start | bytes 196612
  387.0 172.2 %copy-start.4 = (f32[8,96,128]{2,1,0:T(8,128)S(1)}, f32[8,96,128]{2,1,0:T(8,128)}, u32[]{:S(2)}) copy-start(f32[8,96,128]{2,1,0:T(8,128)} %param.11) | copy-start | bytes 1179652
  387.0 172.2 %copy-start.10 = (f32[128,128]{1,0:T(8,128)S(1)}, f32[128,128]{1,0:T(8,128)}, u32[]{:S(2)}) copy-start(f32[128,128]{1,0:T(8,128)} %param.13) | copy-start | bytes 196612
  387.0 175.6 %copy-start.1 = (f32[8,96,128]{2,1,0:T(8,128)S(1)}, f32[8,96,128]{2,1,0:T(8,128)}, u32[]{:S(2)}) copy-start(f32[8,96,128]{2,1,0:T(8,128)} %param.19) | copy-start | bytes 1179652
Sparse Core Ops, SparseCore 0:
  14.0 118.7 all-gather.2
  170.5 73.3 reduce-scatter.2
  250.8 48.0 all-gather.4
  336.3 221.3 reduce-scatter.4
where the time goes:
time: 574 us; the launch traced here: 569 us
  waiting for transfers between devices  371 us (65%)
  matrix products  108 us (19%)
  local copies, waits for them, and re-layouts  43.8 us (8%)
  other arithmetic  32.1 us (6%)
  between operations  14.4 us (3%)
    reduce_scatter x1, waiting for transfers between devices, shards(): lax.psum_scatter(jnp.einsum('ijh,jkh->ikh', picked, right_map, precision=...  164 us
    all_gather x1, waiting for transfers between devices, shards(): whole_left = lax.all_gather(left_local, 'ja', axis=0, tiled=True)  85.2 us
    reduce_scatter x1, waiting for transfers between devices, shards(): lax.psum_scatter(jnp.einsum('ikh,jkh->ijh', picked, right_map, precision=...  73.3 us
    all_gather x1, waiting for transfers between devices, shards(): grad_product = lax.all_gather(own_grad, 'ka', axis=0, tiled=True)  48.2 us
    dot_general x1, matrix products, shards(): jnp.einsum('ikh,jkh->ijh', picked, right_map, precision=lax.Precision.HIG...  22.5 us
    dot_general x1, matrix products, shards(): jnp.einsum('ijh,jkh->ikh', picked, right_map, precision=lax.Precision.HIG...  22.2 us
    dot_general x4, matrix products, project(): jnp.dot(normed, w_gate, precision=lax.Precision.HIGHEST, preferred_elemen...  21.7 us
    dot_general x4, matrix products, project(): jnp.dot(normed, w_value, precision=lax.Precision.HIGHEST, preferred_eleme...  19.9 us
  transfers between devices with their start and end apart: 4, of which 4 were waited for; matrix products, arithmetic and copies ran while one was open for 16% of the time, Pallas kernels for 0%

commit v1 on v0

v1 whole, which is shorter than its diff:
```python
import jax
import jax.numpy as jnp
from jax import lax
from jax.experimental import pallas as pl
from jax.experimental.pallas import tpu as pltpu
from jax.sharding import PartitionSpec as P

f32, bf16 = jnp.float32, jnp.bfloat16
norm_eps = 1e-05

YH, Z, X, YL, CORE = 2, 8, 4, 2, 2
C = 2
NR = 8 // C
HR, QR = NR // 2, NR // 4
CI = 16 * NR
B = 96
T = (B, 128)
MIB = 2**20
MESH = pl.DeviceIdType.MESH
NT = (((1,), (1,)), ((), ()))
NN = (((1,), (0,)), ((), ()))
VM = pl.BlockSpec(memory_space=pltpu.VMEM)
HBM = pl.BlockSpec(memory_space=pl.ANY)


def split(values):
    hi = values.astype(bf16)
    return hi, (values - hi.astype(f32)).astype(bf16)


def dot(a, b, dims=NN):
    return lax.dot_general(a, b, dims, preferred_element_type=f32)


def dot3(a, b, dims=NN):
    a_hi, a_lo = split(a)
    b_hi, b_lo = split(b)
    both = dot(jnp.concatenate([a_hi, a_lo], 1), jnp.concatenate([b_hi, b_hi], dims[0][1][0]), dims)
    return both + dot(a_hi, b_lo, dims)


def mean(values):
    return jnp.mean(values, axis=-1, keepdims=True)


def normalise(values):
    center = values - mean(values)
    scale = lax.rsqrt(mean(center * center) + norm_eps)
    return center * scale, scale


def prepare(gain_col, gate, value, w_up, w_low, wc_hi, wc_lo):
    folded = jnp.concatenate([gate[...] * gain_col[...], value[...] * gain_col[...]], 1)
    hi, lo = split(folded)
    w_up[:128] = hi
    w_up[128:] = hi
    w_low[...] = lo
    if wc_hi is not None:
        hi, lo = split(folded - jnp.mean(folded, axis=0, keepdims=True))
        wc_hi[...] = hi
        wc_lo[...] = lo


def gates(normed, w_up, w_low):
    hi, lo = split(normed)
    both = dot(jnp.concatenate([hi, lo], 1), w_up[...]) + dot(hi, w_low[...])
    return 1.0 / (1.0 + jnp.exp(-both[:, :128])), both[:, 128:]


def forward(values, w_up, w_low):
    s, v = gates(normalise(values)[0], w_up, w_low)
    return s * v


def pull(values, grad, w_up, w_low, wc_hi, wc_lo):
    normed, scale = normalise(values)
    s, v = gates(normed, w_up, w_low)
    d_value = grad * s
    d_gate = d_value * v * (1.0 - s)
    hi, lo = split(jnp.concatenate([d_gate, d_value], 1))
    d = dot(hi, wc_hi[...], NT) + dot(lo, wc_hi[...], NT) + dot(hi, wc_lo[...], NT)
    return scale * (d - normed * mean(d * normed))


def accumulate(dst, src):
    dims = src.shape[:-2]
    if not dims:
        dst[...] = dst[...] + src[...]
        return

    def step(i, _):
        accumulate(dst.at[i], src.at[i])
        return 0

    lax.fori_loop(0, dims[0], step, 0, unroll=True)


def repeat(n, body):
    def step(i, _):
        body(i)
        return 0

    lax.fori_loop(0, n, step, 0, unroll=True)


def run(n, body, events=()):
    def step(t, _):
        for at, event in events:
            pl.when(t == at)(event)
        body(t)
        return 0

    lax.fori_loop(0, n, step, 0)


def rows_in(src, dst, first, n):
    flat = dst.reshape(dst.shape[0] * dst.shape[1], 128)

    def body(u):
        row = first + u
        tile = jnp.concatenate([src[row], jnp.zeros((32, 128), f32)], 0).T
        flat[pl.ds(row, 128, stride=dst.shape[1]), :] = tile

    repeat(n, body)


def rows_out(src, dst, first, n):
    flat = src.reshape(src.shape[0] * src.shape[1], 128)

    def body(u):
        row = first + u
        dst[row] = flat[pl.ds(row, 128, stride=src.shape[1]), :].T[:B]

    repeat(n, body)


class Net:
    def __init__(self, ss, rs):
        self.ss, self.rs = ss, rs
        self.keys, self.sent = {}, []
        ja, ka = lax.axis_index("ja"), lax.axis_index("ka")
        self.yh, self.z = ja // 8, ja % 8
        self.x, self.yl, self.cc = ka // 4, (ka // 2) % 2, ka % 2
        self.yh1, self.yl1, self.cc1 = 1 - self.yh, 1 - self.yl, 1 - self.cc
        self.zs = {d: (self.z + d + 8) % 8 for d in range(-4, 5)}
        self.xs = {d: (self.x + d + 4) % 4 for d in range(-2, 3)}
        self.to = {
            "z+": (self.yh * 8 + self.zs[1], ka),
            "z-": (self.yh * 8 + self.zs[-1], ka),
            "yh": (self.yh1 * 8 + self.z, ka),
            "x+": (ja, self.xs[1] * 4 + ka % 4),
            "x-": (ja, self.xs[-1] * 4 + ka % 4),
            "yl": (ja, self.x * 4 + self.yl1 * 2 + self.cc),
            "cc": (ja, self.x * 4 + self.yl * 2 + self.cc1),
        }

    def greet(self):
        barrier = pltpu.get_barrier_semaphore()
        for dev in self.to.values():
            pl.semaphore_signal(barrier, inc=1, device_id=dev, device_id_type=MESH)
        return lambda: pl.semaphore_wait(barrier, len(self.to))

    def copy(self, src, dst, key, way):
        k = self.keys.setdefault(key, len(self.keys))
        return pltpu.make_async_remote_copy(
            src_ref=src(),
            dst_ref=dst(),
            send_sem=self.ss.at[k],
            recv_sem=self.rs.at[k],
            device_id=self.to[way],
            device_id_type=MESH,
        )

    def send(self, src, dst, key, way):
        self.copy(src, dst, key, way).start()
        self.sent.append((src, dst, key, way))

    def recv(self, dst, key, way):
        self.copy(dst, dst, key, way).wait_recv()

    def drain(self):
        for entry in self.sent:
            self.copy(*entry).wait_send()


ways = ((0, 1, "+"), (1, -1, "-"))


class GatherJa:
    def __init__(self, net, W, c):
        self.n, self.W, self.c = net, W, c

    def at(self, yh, z, lo, hi):
        return lambda: self.W.at[self.c, yh, z, pl.ds(lo, hi - lo)]

    def part(self, stream, d, s):
        if stream == "own":
            return (0, NR) if s < 4 else ((0, HR), (HR, NR))[d]
        return (0, HR) if s < 4 else ((0, QR), (QR, HR))[d]

    def hop(self, stream, d, sign, s):
        n = self.n
        col = n.yh if stream == "own" else n.yh1
        ref = self.at(col, n.zs[-sign * (s - 1)], *self.part(stream, d, s))
        n.send(ref, ref, ("ag", self.c, stream, d, s), "z+" if d == 0 else "z-")

    def got(self, stream, d, sign, s):
        n = self.n
        col = n.yh if stream == "own" else n.yh1
        ref = self.at(col, n.zs[-sign * s], *self.part(stream, d, s))
        n.recv(ref, ("ag", self.c, stream, d, s), "z+" if d == 0 else "z-")

    def over(self, d, sign, s):
        ref = self.at(self.n.yh, self.n.zs[-sign * s], HR, NR)
        self.n.send(ref, ref, ("agy", self.c, d, s), "yh")

    def over_got(self, d, sign, s):
        ref = self.at(self.n.yh1, self.n.zs[-sign * s], HR, NR)
        self.n.recv(ref, ("agy", self.c, d, s), "yh")

    def start(self):
        for d, sign, _ in ways:
            self.hop("own", d, sign, 1)
        ref = self.at(self.n.yh, self.n.z, 0, NR)
        self.n.send(ref, ref, ("agy0", self.c), "yh")

    def start_a(self):
        ref = self.at(self.n.yh1, self.n.z, 0, NR)
        self.n.recv(ref, ("agy0", self.c), "yh")
        for d, sign, _ in ways:
            self.hop("a", d, sign, 1)

    def own(self, s):
        def event():
            for d, sign, _ in ways:
                self.got("own", d, sign, s)
                if s < 4:
                    self.hop("own", d, sign, s + 1)
                    self.over(d, sign, s)
                elif d == 1:
                    self.over(d, sign, s)

        return event

    def a(self, s):
        def event():
            for d, sign, _ in ways:
                self.got("a", d, sign, s)
                if s < 4:
                    self.hop("a", d, sign, s + 1)

        return event

    def finish(self):
        for s in range(1, 4):
            for d, sign, _ in ways:
                self.over_got(d, sign, s)
        self.over_got(1, -1, 4)


class ScatterKa:
    def __init__(self, net, Pn, Q, bufs, c):
        self.n, self.Pn, self.Q, self.c = net, Pn, Q, c
        self.x1a, self.x1b, self.y2, self.x2a, self.x2b, self.y1 = bufs

    def start(self):
        n, c = self.n, self.c
        n.send(lambda: self.Pn.at[c, :, :, n.cc1], lambda: self.Q.at[c], ("core", c), "cc")

    def q(self, x, yl, lo, hi):
        if yl is None:
            return lambda: self.Q.at[self.c, x, :, pl.ds(lo, hi - lo)]
        return lambda: self.Q.at[self.c, x, yl, pl.ds(lo, hi - lo)]

    def one(self):
        n, c = self.n, self.c
        n.recv(lambda: self.Q.at[c], ("core", c), "cc")
        accumulate(self.Q.at[c], self.Pn.at[c, :, :, n.cc])
        n.send(lambda: self.Q.at[c, :, n.yl1, pl.ds(HR, HR)], lambda: self.y2.at[c], ("y2", c), "yl")
        for d, sign, w in ways:
            n.send(self.q(n.xs[2], None, d * QR, d * QR + QR), lambda: self.x1a.at[c, d], ("x1a", c, d), "x" + w)

    def two(self):
        n, c = self.n, self.c
        for d, sign, w in ways:
            n.recv(lambda: self.x1a.at[c, d], ("x1a", c, d), "x" + w)
            accumulate(self.q(n.xs[sign], None, d * QR, d * QR + QR)(), self.x1a.at[c, d])
            n.send(self.q(n.xs[sign], None, 0, HR), lambda: self.x1b.at[c, d], ("x1b", c, d), "x" + w)

    def three(self):
        n, c = self.n, self.c
        n.recv(lambda: self.y2.at[c], ("y2", c), "yl")
        accumulate(self.Q.at[c, :, n.yl, pl.ds(HR, HR)], self.y2.at[c])
        for d, sign, w in ways:
            lo = HR + d * QR
            n.send(self.q(n.xs[2], n.yl, lo, lo + QR), lambda: self.x2a.at[c, d], ("x2a", c, d), "x" + w)

    def four(self):
        n, c = self.n, self.c
        for d, sign, w in ways:
            n.recv(lambda: self.x1b.at[c, d], ("x1b", c, d), "x" + w)
            accumulate(self.q(n.x, None, 0, HR)(), self.x1b.at[c, d])
        n.send(self.q(n.x, n.yl1, 0, HR), lambda: self.y1.at[c], ("y1", c), "yl")

    def five(self):
        n, c = self.n, self.c
        for d, sign, w in ways:
            lo = HR + d * QR
            n.recv(lambda: self.x2a.at[c, d], ("x2a", c, d), "x" + w)
            accumulate(self.q(n.xs[sign], n.yl, lo, lo + QR)(), self.x2a.at[c, d])
            n.send(self.q(n.xs[sign], n.yl, HR, NR), lambda: self.x2b.at[c, d], ("x2b", c, d), "x" + w)

    def six(self):
        n, c = self.n, self.c
        n.recv(lambda: self.y1.at[c], ("y1", c), "yl")
        accumulate(self.q(n.x, n.yl, 0, HR)(), self.y1.at[c])
        for d, sign, w in ways:
            n.recv(lambda: self.x2b.at[c, d], ("x2b", c, d), "x" + w)
            accumulate(self.q(n.x, n.yl, HR, NR)(), self.x2b.at[c, d])


class GatherKa:
    def __init__(self, net, G, c):
        self.n, self.G, self.c = net, G, c

    def g(self, x, yl, core, lo, hi):
        if yl is None:
            return lambda: self.G.at[self.c, x, :, core, pl.ds(lo, hi - lo)]
        return lambda: self.G.at[self.c, x, yl, core, pl.ds(lo, hi - lo)]

    def put(self, key, way, *where):
        ref = self.g(*where)
        self.n.send(ref, ref, ("agk", self.c) + key, way)

    def get(self, key, way, *where):
        self.n.recv(self.g(*where), ("agk", self.c) + key, way)

    def zero(self):
        n = self.n
        self.put(("y1",), "yl", n.x, n.yl, n.cc, 0, HR)
        for d, sign, w in ways:
            self.put(("x2", d), "x" + w, n.x, n.yl, n.cc, HR, NR)
        self.put(("c0",), "cc", n.x, n.yl, n.cc, 0, NR)
        self.put(("y2", 0), "yl", n.x, n.yl, n.cc, HR, NR)

    def one(self):
        n = self.n
        self.get(("y1",), "yl", n.x, n.yl1, n.cc, 0, HR)
        for d, sign, w in ways:
            self.put(("x1", d), "x" + w, n.x, None, n.cc, 0, HR)
        self.put(("c1",), "cc", n.x, n.yl1, n.cc, 0, HR)

    def two(self):
        n = self.n
        for d, sign, w in ways:
            src = n.xs[-sign]
            self.get(("x2", d), "x" + w, src, n.yl, n.cc, HR, NR)
            self.put(("x2h", d), "x" + w, src, n.yl, n.cc, HR + d * QR, HR + d * QR + QR)
            self.put(("y2", 1 + d), "yl", src, n.yl, n.cc, HR, NR)
            self.put(("c2", d), "cc", src, n.yl, n.cc, HR, NR)

    def three(self):
        n = self.n
        for d, sign, w in ways:
            src = n.xs[-sign]
            self.get(("x1", d), "x" + w, src, None, n.cc, 0, HR)
            self.put(("x1h", d), "x" + w, src, None, n.cc, d * QR, d * QR + QR)
            self.put(("c3", d), "cc", src, None, n.cc, 0, HR)

    def four(self):
        n = self.n
        for d, sign, w in ways:
            self.get(("x2h", d), "x" + w, n.xs[2], n.yl, n.cc, HR + d * QR, HR + d * QR + QR)
        self.put(("y2", 3), "yl", n.xs[2], n.yl, n.cc, HR, NR)
        self.put(("c4",), "cc", n.xs[2], n.yl, n.cc, HR, NR)
        for d, sign, w in ways:
            src = n.xs[-sign]
            self.get(("y2", 1 + d), "yl", src, n.yl1, n.cc, HR, NR)
            self.put(("c6", 1 + d), "cc", src, n.yl1, n.cc, HR, NR)
        self.get(("y2", 0), "yl", n.x, n.yl1, n.cc, HR, NR)
        self.put(("c6", 0), "cc", n.x, n.yl1, n.cc, HR, NR)

    def five(self):
        n = self.n
        for d, sign, w in ways:
            self.get(("x1h", d), "x" + w, n.xs[2], None, n.cc, d * QR, d * QR + QR)
        self.put(("c5",), "cc", n.xs[2], None, n.cc, 0, HR)
        self.get(("y2", 3), "yl", n.xs[2], n.yl1, n.cc, HR, NR)
        self.put(("c6", 3), "cc", n.xs[2], n.yl1, n.cc, HR, NR)

    def finish(self):
        n = self.n
        o = n.cc1
        self.get(("c0",), "cc", n.x, n.yl, o, 0, NR)
        self.get(("c1",), "cc", n.x, n.yl1, o, 0, HR)
        for d, sign, w in ways:
            src = n.xs[-sign]
            self.get(("c2", d), "cc", src, n.yl, o, HR, NR)
            self.get(("c3", d), "cc", src, None, o, 0, HR)
            self.get(("c6", 1 + d), "cc", src, n.yl1, o, HR, NR)
        self.get(("c4",), "cc", n.xs[2], n.yl, o, HR, NR)
        self.get(("c5",), "cc", n.xs[2], None, o, 0, HR)
        self.get(("c6", 0), "cc", n.x, n.yl1, o, HR, NR)
        self.get(("c6", 3), "cc", n.xs[2], n.yl1, o, HR, NR)


class ScatterJa:
    def __init__(self, net, N, bufs, c):
        self.n, self.N, self.c = net, N, c
        self.ry, self.ra1, self.ra, self.rb1, self.rb, self.rf = bufs

    def rows(self, stream, d, s):
        lo = 0 if stream == "a" else HR
        return (lo, lo + HR) if s > 1 else (lo + d * QR, lo + d * QR + QR)

    def block(self, stream, z, lo, hi):
        if stream == "a":
            return lambda: self.N.at[self.c, :, z, pl.ds(lo, hi - lo)]
        return lambda: self.N.at[self.c, self.n.yh, z, pl.ds(lo, hi - lo)]

    def land(self, stream, d, s):
        first, rest = (self.ra1, self.ra) if stream == "a" else (self.rb1, self.rb)
        if s == 1:
            return lambda: first.at[self.c, d]
        return lambda: rest.at[self.c, d, s - 2]

    def push(self, stream, d, sign, w, s):
        src = self.block(stream, self.n.zs[sign * (5 - s)], *self.rows(stream, d, s))
        self.n.send(src, self.land(stream, d, s), ("rs", self.c, stream, d, s), "z" + w)

    def take(self, stream, d, sign, w, s):
        land = self.land(stream, d, s)
        self.n.recv(land, ("rs", self.c, stream, d, s), "z" + w)
        dst = self.block(stream, self.n.zs[sign * (4 - s)], *self.rows(stream, d, s))
        accumulate(dst(), land())

    def start(self):
        n, c = self.n, self.c
        n.send(lambda: self.N.at[c, n.yh1, :, pl.ds(HR, HR)], lambda: self.ry.at[c], ("rsy", c), "yh")
        for d, sign, w in ways:
            self.push("a", d, sign, w, 1)

    def start_b(self):
        n, c = self.n, self.c
        n.recv(lambda: self.ry.at[c], ("rsy", c), "yh")
        accumulate(self.N.at[c, n.yh, :, pl.ds(HR, HR)], self.ry.at[c])
        for d, sign, w in ways:
            self.push("b", d, sign, w, 1)

    def step(self, stream, s):
        def event():
            for d, sign, w in ways:
                self.take(stream, d, sign, w, s)
                if s < 4:
                    self.push(stream, d, sign, w, s + 1)
            if s == 4 and stream == "a":
                self.n.send(
                    lambda: self.N.at[self.c, self.n.yh1, self.n.z, pl.ds(0, HR)],
                    lambda: self.rf.at[self.c],
                    ("rsf", self.c),
                    "yh",
                )

        return event

    def finish(self):
        n, c = self.n, self.c
        n.recv(lambda: self.rf.at[c], ("rsf", c), "yh")
        accumulate(N_at(self.N, c, n, 0, HR), self.rf.at[c])


def N_at(N, c, n, lo, hi):
    return N.at[c, n.yh, n.z, pl.ds(lo, hi - lo)]


def first_kernel(
    pair, slab, gain_col, left_gate, left_value, right_gate, right_value, out_gain, out_weight, cot,
    update, own_grad, right_out, left_out,
    xv, wl_up, wl_low, wr_up, wr_low, W, Rt, Lt, Hb, Pn, Q, x1a, x1b, y2, x2a, x2b, y1, ss, rs, local,
):
    net = Net(ss, rs)
    entered = net.greet()
    load = pltpu.make_async_copy(pair, xv, local.at[0])
    load.start()
    prepare(gain_col, left_gate, left_value, wl_up, wl_low, None, None)
    ag = [GatherJa(net, W, c) for c in range(C)]
    rk = [ScatterKa(net, Pn, Q, (x1a, x1b, y2, x2a, x2b, y1), c) for c in range(C)]

    for c in range(C):
        own = forward(slab[c * NR : (c + 1) * NR].reshape(NR * B, 128), wl_up, wl_low)
        W[c, net.yh, net.z] = own.reshape(NR, B, 128)
        if c == 0:
            entered()
            ag[0].start()
    prepare(gain_col, right_gate, right_value, wr_up, wr_low, None, None)
    load.wait()

    flat_R = Rt.reshape(128 * B, 128)

    def right_step(t):
        G = 4
        made = forward(xv[pl.ds(t * G, G)].reshape(G * B, 128), wr_up, wr_low)
        for u in range(G):
            tile = jnp.concatenate([made[u * B : (u + 1) * B], jnp.zeros((32, 128), f32)], 0).T
            flat_R[pl.ds(t * G + u, 128, stride=B), :] = tile

    a0 = ag[0]
    run(24, right_step, [(4, a0.start_a), (7, a0.own(1)), (9, a0.a(1)), (14, a0.own(2)), (16, a0.a(2)), (22, a0.own(3))])
    save_right = pltpu.make_async_copy(Rt, right_out, local.at[1])
    save_right.start()
    a0.a(3)()

    Wf = W.reshape(C * 16 * NR, B, 128)

    def turn_left(c, lo, hi, events=()):
        base = c * CI + lo
        run((hi - lo) // 8, lambda t: rows_in(Wf, Lt, base + t * 8, 8), events)

    def product(c, events=()):
        def body(t):
            def one(u):
                h = t * 8 + u
                Hb[h, c * CI : (c + 1) * CI, :B] = dot3(Lt[h, c * CI : (c + 1) * CI, :], Rt[h], NT)

            repeat(8, one)

        run(16, body, events)

    Pf = Pn.reshape(C * 16 * NR, B, 128)

    def turn_product(c, events=()):
        run(CI // 8, lambda t: rows_out(Hb, Pf, c * CI + t * 8, 8), events)

    def finish_rows(c):
        def body(u):
            r = c * NR + u
            normed, scale = normalise(Q[c, net.x, net.yl, u])
            update[r] = dot3(normed * out_gain[...], out_weight[...])
            d = dot3(cot[r], out_weight[...], NT) * out_gain[...]
            own_grad[r] = scale * (d - mean(d) - normed * mean(d * normed))

        run(NR, body)

    if C == 1:
        a0.own(4)()
        a0.a(4)()
        a0.finish()
        turn_left(0, 0, CI)
        product(0)
        turn_product(0)
    else:
        a1 = ag[1]
        a1.start()
        a0.own(4)()
        a0.a(4)()
        a0.finish()
        turn_left(0, 0, CI, [(2, a1.start_a)])
        a1.own(1)()
        product(0, [(3, a1.a(1)), (9, a1.own(2)), (13, a1.a(2))])
        turn_product(0)
        rk[0].start()
        a1.own(3)()
        rk[0].one()
        a1.a(3)()
        rk[0].two()
        rk[0].three()
        a1.own(4)()
        a1.a(4)()
        a1.finish()
        turn_left(1, 0, CI, [(3, rk[0].four), (6, rk[0].five)])
        product(1, [(6, rk[0].six)])
        turn_product(1)
    save_left = pltpu.make_async_copy(Lt, left_out, local.at[2])
    save_left.start()
    last = rk[C - 1]
    last.start()
    if C == 2:
        finish_rows(0)
    last.one()
    last.two()
    last.three()
    last.four()
    last.five()
    last.six()
    finish_rows(C - 1)
    net.drain()
    save_right.wait()
    save_left.wait()


def second_kernel(
    pair, slab, gain_col, left_gate, left_value, right_gate, right_value, own_grad, right_in, left_in,
    grad_pair, grad_slab,
    xv, wl_up, wl_low, wlc_hi, wlc_lo, wr_up, wr_low, wrc_hi, wrc_lo,
    Rt, Lt, G, Gt, Hb, N, ry, ra1, ra, rb1, rb, rf, ss, rs, local,
):
    net = Net(ss, rs)
    entered = net.greet()
    loads = [
        pltpu.make_async_copy(right_in, Rt, local.at[0]),
        pltpu.make_async_copy(left_in, Lt, local.at[1]),
        pltpu.make_async_copy(pair, xv, local.at[2]),
    ]
    for load in loads:
        load.start()
    gk = [GatherKa(net, G, c) for c in range(C)]
    sj = [ScatterJa(net, N, (ry, ra1, ra, rb1, rb, rf), c) for c in range(C)]
    for c in range(C):
        G[c, net.x, net.yl, net.cc] = own_grad[c * NR : (c + 1) * NR]
    entered()
    g0 = gk[0]
    g0.zero()
    prepare(gain_col, left_gate, left_value, wl_up, wl_low, wlc_hi, wlc_lo)
    prepare(gain_col, right_gate, right_value, wr_up, wr_low, wrc_hi, wrc_lo)
    g0.one()
    g0.two()
    g0.three()
    if C == 2:
        gk[1].zero()
    g0.four()
    g0.five()
    g0.finish()
    for load in loads:
        load.wait()

    Gf = G.reshape(C * 16 * NR, B, 128)
    Nf = N.reshape(C * 16 * NR, B, 128)

    def turn_grad(c, events=()):
        run(CI // 8, lambda t: rows_in(Gf, Gt, c * CI + t * 8, 8), events)

    def left_product(c, events=()):
        def body(t):
            def one(u):
                h = t * 8 + u
                right = jnp.concatenate([Rt[h], jnp.zeros((32, 128), f32)], 0)
                Hb[h, c * CI : (c + 1) * CI, :] = dot3(Gt[h, c * CI : (c + 1) * CI, :], right)

            repeat(8, one)

        run(16, body, events)

    def turn_back(c, events=()):
        run(CI // 8, lambda t: rows_out(Hb, Nf, c * CI + t * 8, 8), events)

    def right_product(events=()):
        def body(t):
            def one(u):
                h = t * 8 + u
                Hb[h, :B, :] = dot3(Gt[h].T, Lt[h])[:B]

            repeat(8, one)

        run(16, body, events)

    flat_H = Hb.reshape(128 * 128, 128)

    def right_pull(events=()):
        K = 4

        def body(t):
            grads = jnp.concatenate(
                [flat_H[pl.ds(t * K + u, 128, stride=128), :].T[:B] for u in range(K)], 0
            )
            out = pull(xv[pl.ds(t * K, K)].reshape(K * B, 128), grads, wr_up, wr_low, wrc_hi, wrc_lo)
            grad_pair[pl.ds(t * K, K)] = out.reshape(K, B, 128)

        run(24, body, events)

    def left_pull(c):
        grads = N[c, net.yh, net.z].reshape(NR * B, 128)
        out = pull(slab[c * NR : (c + 1) * NR].reshape(NR * B, 128), grads, wl_up, wl_low, wlc_hi, wlc_lo)
        grad_slab[c * NR : (c + 1) * NR] = out.reshape(NR, B, 128)

    if C == 1:
        turn_grad(0)
        left_product(0)
        turn_back(0)
        s = sj[0]
        s.start()
        right_product([(8, s.step("a", 1))])
        right_pull([(0, s.step("a", 2)), (8, s.step("a", 3)), (16, s.step("a", 4))])
        s.start_b()
        for k in range(1, 5):
            s.step("b", k)()
        s.finish()
        left_pull(0)
    else:
        g1 = gk[1]
        turn_grad(0, [(2, g1.one), (5, g1.two)])
        left_product(0, [(2, g1.three), (10, g1.four)])
        turn_back(0, [(4, g1.five)])
        s, e = sj
        s.start()
        g1.finish()
        turn_grad(1, [(4, s.step("a", 1))])
        left_product(1, [(4, s.step("a", 2)), (13, s.step("a", 3))])
        turn_back(1, [(3, s.start_b)])
        s.step("a", 4)()
        e.start()
        right_product(
            [(2, s.step("b", 1)), (5, s.step("b", 2)), (8, s.step("b", 3)), (11, e.step("a", 1)), (13, s.step("b", 4))]
        )
        right_pull(
            [(0, s.finish), (1, e.step("a", 2)), (7, e.step("a", 3)), (10, e.start_b), (13, e.step("a", 4)),
             (16, e.step("b", 1)), (19, e.step("b", 2)), (22, e.step("b", 3))]
        )
        left_pull(0)
        e.step("b", 4)()
        e.finish()
        left_pull(1)
    net.drain()


def shards(
    pair_map, slab_rows, norm_gain, left_gate, left_value, right_gate, right_value, out_gain, out_weight, cotangent
):
    S = jax.ShapeDtypeStruct
    V = pltpu.VMEM
    weights = [V((256, 256), bf16), V((128, 256), bf16)]
    gain_col = norm_gain.reshape(128, 1)
    update, own_grad, right_turned, left_turned = pl.pallas_call(
        first_kernel,
        out_shape=[S((8,) + T, f32), S((8,) + T, f32), S((128, B, 128), f32), S((128, 128, 128), f32)],
        in_specs=[HBM] + [VM] * 9,
        out_specs=[VM, VM, HBM, HBM],
        scratch_shapes=[V((B,) + T, f32)]
        + weights * 2
        + [
            V((C, YH, Z, NR) + T, f32),
            V((128, B, 128), f32),
            V((128, 128, 128), f32),
            V((128, 128, 128), f32),
            V((C, X, YL, CORE, NR) + T, f32),
            V((C, X, YL, NR) + T, f32),
            V((C, 2, YL, QR) + T, f32),
            V((C, 2, YL, HR) + T, f32),
            V((C, X, HR) + T, f32),
            V((C, 2, QR) + T, f32),
            V((C, 2, HR) + T, f32),
            V((C, HR) + T, f32),
            pltpu.SemaphoreType.DMA((80,)),
            pltpu.SemaphoreType.DMA((80,)),
            pltpu.SemaphoreType.DMA((3,)),
        ],
        compiler_params=pltpu.CompilerParams(collective_id=1, has_side_effects=True, vmem_limit_bytes=60 * MIB),
        name="first",
    )(
        pair_map, slab_rows, gain_col, left_gate, left_value, right_gate, right_value,
        out_gain.reshape(1, 128), out_weight, cotangent,
    )
    grad_pair, grad_slab = pl.pallas_call(
        second_kernel,
        out_shape=[S((B,) + T, f32), S((8,) + T, f32)],
        in_specs=[HBM] + [VM] * 7 + [HBM] * 2,
        out_specs=[VM, VM],
        scratch_shapes=[V((B,) + T, f32)]
        + (weights + [V((128, 256), bf16)] * 2) * 2
        + [
            V((128, B, 128), f32),
            V((128, 128, 128), f32),
            V((C, X, YL, CORE, NR) + T, f32),
            V((128, 128, 128), f32),
            V((128, 128, 128), f32),
            V((C, YH, Z, NR) + T, f32),
            V((C, Z, HR) + T, f32),
            V((C, 2, YH, QR) + T, f32),
            V((C, 2, 3, YH, HR) + T, f32),
            V((C, 2, QR) + T, f32),
            V((C, 2, 3, HR) + T, f32),
            V((C, HR) + T, f32),
            pltpu.SemaphoreType.DMA((96,)),
            pltpu.SemaphoreType.DMA((96,)),
            pltpu.SemaphoreType.DMA((3,)),
        ],
        compiler_params=pltpu.CompilerParams(collective_id=2, has_side_effects=True, vmem_limit_bytes=62 * MIB),
        name="second",
    )(pair_map, slab_rows, gain_col, left_gate, left_value, right_gate, right_value, own_grad, right_turned, left_turned)
    return (update, grad_pair, grad_slab)


def solution(mesh):
    in_specs = (
        P("ja", "ka", None),
        P("ja", "ka", None),
        P(),
        P(),
        P(),
        P(),
        P(),
        P(),
        P(),
        P("ka", "ja", None),
    )
    out_specs = (P("ka", "ja", None), P("ja", "ka", None), P("ja", "ka", None))
    return jax.shard_map(shards, mesh=mesh, in_specs=in_specs, out_specs=out_specs, check_vma=False)
```

time: 574 us -> 242 us (0.42)
  waiting for transfers between devices: 371 us -> 0 us
  Pallas kernels: 0 us -> 233 us
  matrix products: 108 us -> 0 us
  local copies, waits for them, and re-layouts: 43.8 us -> 7.79 us
  other arithmetic: 32.1 us -> 0 us
  between operations: 14.4 us -> 0.66 us
    reduce_scatter x2 -> x0, waiting for transfers between devices: 237 us -> none  [the longest x1 164 us: shards(): lax.psum_scatter(jnp.einsum('ijh,jkh->ikh', picked, right_map, precision=...]
    pallas_call x0 -> x2, Pallas kernels: none -> 233 us  [the longest x1 118 us: shards(): pl.pallas_call(first_kernel, out_shape=[S((8,) + T, f32), S((8,) + T, f32...]
    all_gather x2 -> x0, waiting for transfers between devices: 133 us -> none  [the longest x1 85.2 us: shards(): whole_left = lax.all_gather(left_local, 'ja', axis=0, tiled=True)]
    dot_general x13 -> x0, matrix products: 108 us -> none  [the longest x1 22.5 us: shards(): jnp.einsum('ikh,jkh->ijh', picked, right_map, precision=lax.Precision.HIG...]
    reduce_sum x8 -> x0, other arithmetic: 21.9 us -> none  [the longest x6 14.9 us: layer_norm(): center = values - jnp.mean(values, axis=-1, keepdims=True)]
    all_gather x2 -> x0, local copies, waits for them, and re-layouts: 16.8 us -> none  [the longest x1 8.43 us: shards(): whole_left = lax.all_gather(left_local, 'ja', axis=0, tiled=True)]
    dot_general x2 -> x0, local copies, waits for them, and re-layouts: 12.9 us -> none  [the longest x1 6.67 us: shards(): jnp.einsum('ijh,jkh->ikh', picked, right_map, precision=lax.Precision.HIG...]
    add_any x3 -> x0, other arithmetic: 10.1 us -> none  [layer_norm(): center = values - jnp.mean(values, axis=-1, keepdims=True)]
  transfers between devices with their start and end apart: 4 -> 0, of which waited for: 4 -> 0; matrix products, arithmetic and copies ran while one was open for 16% -> 0% of each run, Pallas kernels for 0% -> 0%
where the time goes in v1:
time: 242 us; the launch traced here: 241 us
  Pallas kernels  233 us (96%)
  local copies, waits for them, and re-layouts  7.79 us (3%)
    pallas_call x1, Pallas kernels, shards(): pl.pallas_call(first_kernel, out_shape=[S((8,) + T, f32), S((8,) + T, f32...  118 us
    pallas_call x1, Pallas kernels, shards(): pl.pallas_call(second_kernel, out_shape=[S((B,) + T, f32), S((8,) + T, f3...  114 us
    unnamed x7, local copies, waits for them, and re-layouts  6.4 us

profile of v1, /device:TPU:2, one launch (start us, length us, event | category | flops | bytes accessed | tf_op | source)
XLA Modules:
  0.0 241.0 jit_solution(17377861493479119619)
XLA Ops:
  0.6 1.4 copy.13.gain_col
  2.0 118.1 %first.1 = (f32[8,96,128]{2,1,0:T(8,128)}, f32[8,96,128]{2,1,0:T(8,128)}, f32[128,96,128]{2,1,0:T(8,128)}, f32[128,128,128]{2,1,0:T(8,128)}) custom-call(f32[96,96,128]{2,1,0:T(8,128)} %pair.3, f32[8,96,128]{2,1,0:T(8,128)} %slab.3, f32[128,1]{1,0:T(8,128)} %copy.13.gain_col, f32[128,128]{1,0:T(8,128)} %left_gate.3, f32[128,128]{1,0:T(8,128)} %left_value.3, ...), custom_call_target="tpu_custom_call" | custom-call | tf_op jit(solution)/shard_map/first/pallas_call | solution.py:722
  120.1 0.0 copy-start
  120.1 114.5 %second.1 = (f32[96,96,128]{2,1,0:T(8,128)}, f32[8,96,128]{2,1,0:T(8,128)}) custom-call(f32[96,96,128]{2,1,0:T(8,128)} %pair.3, f32[8,96,128]{2,1,0:T(8,128)} %slab.3, f32[128,1]{1,0:T(8,128)} %copy.13.gain_col, f32[128,128]{1,0:T(8,128)} %left_gate.3, f32[128,128]{1,0:T(8,128)} %left_value.3, f32[128,128]{1,0:T(8,128)} %right_gate.3, ...), custom_call_target="tpu_custom_call" | custom-call | tf_op jit(solution)/shard_map/second/pallas_call | solution.py:752
  234.6 0.0 copy-done
  234.6 0.7 copy.18
  235.4 0.0 copy-start.1
  235.4 4.9 %copy.19 = f32[96,96,128]{2,1,0:T(8,128)} copy(f32[96,96,128]{2,1,0:T(8,128)} %get-tuple-element.19) | data formatting | bytes 9437184
  240.3 0.0 copy-done.1
  240.3 0.7 copy.20
Async XLA Ops:
  120.1 114.5 %copy-start = (f32[8,96,128]{2,1,0:T(8,128)S(1)}, f32[8,96,128]{2,1,0:T(8,128)}, u32[]{:S(2)}) copy-start(f32[8,96,128]{2,1,0:T(8,128)} %get-tuple-element.18) | copy-start | bytes 1179652
  235.4 4.9 %copy-start.1 = (f32[8,96,128]{2,1,0:T(8,128)S(1)}, f32[8,96,128]{2,1,0:T(8,128)}, u32[]{:S(2)}) copy-start(f32[8,96,128]{2,1,0:T(8,128)} %get-tuple-element.20) | copy-start | bytes 1179652

commit v2 on v0

v2 whole, which is shorter than its diff:
```python
import jax
import jax.numpy as jnp
from jax import lax
from jax.experimental import pallas as pl
from jax.experimental.pallas import tpu as pltpu
from jax.sharding import PartitionSpec as P

f32, bf16 = jnp.float32, jnp.bfloat16
norm_eps = 1e-05

YH, Z, X, YL, CORE = 2, 8, 4, 2, 2
C = 2
NR = 8 // C
HR, QR = NR // 2, NR // 4
KR = (2, 2)
KG = (2, 2)
CI = 16 * NR
B = 96
T = (B, 128)
MIB = 2**20
MESH = pl.DeviceIdType.MESH
NT = (((1,), (1,)), ((), ()))
NN = (((1,), (0,)), ((), ()))
VM = pl.BlockSpec(memory_space=pltpu.VMEM)
HBM = pl.BlockSpec(memory_space=pl.ANY)


def split(values):
    hi = values.astype(bf16)
    return hi, (values - hi.astype(f32)).astype(bf16)


def dot(a, b, dims=NN):
    return lax.dot_general(a, b, dims, preferred_element_type=f32)


def dot3(a, b, dims=NN):
    a_hi, a_lo = split(a)
    b_hi, b_lo = split(b)
    both = dot(jnp.concatenate([a_hi, a_lo], 1), jnp.concatenate([b_hi, b_hi], dims[0][1][0]), dims)
    return both + dot(a_hi, b_lo, dims)


def mean(values):
    return jnp.mean(values, axis=-1, keepdims=True)


def normalise(values):
    center = values - mean(values)
    scale = lax.rsqrt(mean(center * center) + norm_eps)
    return center * scale, scale


def prepare(gain, gate, value, w_up, w_low, wc_hi, wc_lo):
    column = jnp.broadcast_to(gain[...], (128, 128)).T
    folded = jnp.concatenate([gate[...] * column, value[...] * column], 1)
    hi, lo = split(folded)
    w_up[:128] = hi
    w_up[128:] = hi
    w_low[...] = lo
    hi, lo = split(folded - jnp.mean(folded, axis=0, keepdims=True))
    wc_hi[...] = hi
    wc_lo[...] = lo


def gates(normed, w_up, w_low):
    hi, lo = split(normed)
    both = dot(jnp.concatenate([hi, lo], 1), w_up[...]) + dot(hi, w_low[...])
    return 1.0 / (1.0 + jnp.exp(-both[:, :128])), both[:, 128:]


def forward(values, w_up, w_low):
    s, v = gates(normalise(values)[0], w_up, w_low)
    return s * v


def pull(values, grad, w_up, w_low, wc_hi, wc_lo):
    normed, scale = normalise(values)
    s, v = gates(normed, w_up, w_low)
    d_value = grad * s
    d_gate = d_value * v * (1.0 - s)
    hi, lo = split(jnp.concatenate([d_gate, d_value], 1))
    d = dot(hi, wc_hi[...], NT) + dot(lo, wc_hi[...], NT) + dot(hi, wc_lo[...], NT)
    return scale * (d - normed * mean(d * normed))


def accumulate(dst, src):
    dims = src.shape[:-2]
    if not dims:
        dst[...] = dst[...] + src[...]
        return

    def step(i, _):
        accumulate(dst.at[i], src.at[i])
        return 0

    lax.fori_loop(0, dims[0], step, 0, unroll=True)


def repeat(n, body):
    def step(i, _):
        body(i)
        return 0

    lax.fori_loop(0, n, step, 0, unroll=True)


def run(n, body, events=()):
    def step(t, _):
        for at, event in events:
            pl.when(t == at)(event)
        body(t)
        return 0

    lax.fori_loop(0, n, step, 0)


def rows_in(src, dst, first, n):
    flat = dst.reshape(dst.shape[0] * dst.shape[1], 128)

    def body(u):
        row = first + u
        tile = jnp.concatenate([src[row], jnp.zeros((32, 128), f32)], 0).T
        flat[pl.ds(row, 128, stride=dst.shape[1]), :] = tile

    repeat(n, body)


def rows_out(src, dst, first, n):
    flat = src.reshape(src.shape[0] * src.shape[1], 128)

    def body(u):
        row = first + u
        dst[row] = flat[pl.ds(row, 128, stride=src.shape[1]), :].T[:B]

    repeat(n, body)


class Net:
    def __init__(self, ss, rs):
        self.ss, self.rs = ss, rs
        self.keys, self.sent = {}, []
        ja, ka = lax.axis_index("ja"), lax.axis_index("ka")
        self.yh, self.z = ja // 8, ja % 8
        self.x, self.yl, self.cc = ka // 4, (ka // 2) % 2, ka % 2
        self.yh1, self.yl1, self.cc1 = 1 - self.yh, 1 - self.yl, 1 - self.cc
        self.zs = {d: by_z((self.z + d + 8) % 8) for d in range(-4, 5)}
        z_at = {d: (self.z + d + 8) % 8 for d in (-1, 1)}
        self.xs = {d: by_x((self.x + d + 4) % 4) for d in range(-2, 3)}
        x_at = {d: (self.x + d + 4) % 4 for d in (-1, 1)}
        self.to = {
            "z+": (self.yh * 8 + z_at[1], ka),
            "z-": (self.yh * 8 + z_at[-1], ka),
            "yh": (self.yh1 * 8 + self.z, ka),
            "x+": (ja, x_at[1] * 4 + ka % 4),
            "x-": (ja, x_at[-1] * 4 + ka % 4),
            "yl": (ja, self.x * 4 + self.yl1 * 2 + self.cc),
            "cc": (ja, self.x * 4 + self.yl * 2 + self.cc1),
        }

    def greet(self):
        barrier = pltpu.get_barrier_semaphore()
        for dev in self.to.values():
            pl.semaphore_signal(barrier, inc=1, device_id=dev, device_id_type=MESH)
        return lambda: pl.semaphore_wait(barrier, len(self.to))

    def copy(self, src, dst, key, way):
        k = self.keys.setdefault(key, len(self.keys))
        return pltpu.make_async_remote_copy(
            src_ref=src(),
            dst_ref=dst(),
            send_sem=self.ss.at[k],
            recv_sem=self.rs.at[k],
            device_id=self.to[way],
            device_id_type=MESH,
        )

    def send(self, src, dst, key, way):
        self.copy(src, dst, key, way).start()
        self.sent.append((src, dst, key, way))

    def recv(self, dst, key, way):
        self.copy(dst, dst, key, way).wait_recv()

    def drain(self, *kinds):
        for entry in [e for e in self.sent if not kinds or e[2][:2] in kinds]:
            self.copy(*entry).wait_send()
            self.sent.remove(entry)


ways = ((0, 1, "+"), (1, -1, "-"))


def by_z(z):
    return z // 4, (z // 2) % 2, z % 2


def by_x(x):
    return x // 2, x % 2


def UP(rows):
    return (rows + 1) // 2


def halves(lo, hi):
    mid = (lo + hi) // 2
    return (lo, mid), (mid, hi)


U, V = (0, HR), (HR, NR)
streams = {"u": U, "v": V, "a": U}


def rows_of(stream, d, end):
    return halves(*streams[stream])[d] if end else streams[stream]


class GatherJa:
    def __init__(self, net, W, c):
        self.n, self.W, self.c = net, W, c

    def at(self, yh, z, lo, hi):
        return lambda: self.W.at[(self.c, yh) + z + (pl.ds(lo, hi - lo),)]

    def piece(self, stream, d, z, s):
        return self.at(self.n.yh1 if stream == "a" else self.n.yh, z, *rows_of(stream, d, s == 4))

    def hop(self, stream, s):
        for d, sign, w in ways:
            ref = self.piece(stream, d, self.n.zs[-sign * (s - 1)], s)
            self.n.send(ref, ref, ("ag", self.c, stream, d, s), "z" + w)

    def over(self, d, rows):
        ref = self.at(self.n.yh, self.n.zs[d], *rows)
        self.n.send(ref, ref, ("agy", self.c, d, rows), "yh")

    def over_got(self, d, rows):
        self.n.recv(self.at(self.n.yh1, self.n.zs[d], *rows), ("agy", self.c, d, rows), "yh")

    def start(self):
        self.hop("u", 1)
        self.over(0, U)
        self.hop("v", 1)
        self.over(0, V)

    def start_a(self):
        self.over_got(0, U)
        self.hop("a", 1)

    def step(self, stream, s):
        def event():
            for d, sign, w in ways:
                ref = self.piece(stream, d, self.n.zs[-sign * s], s)
                self.n.recv(ref, ("ag", self.c, stream, d, s), "z" + w)
            if s < 4:
                self.hop(stream, s + 1)
            if stream == "v":
                for d in (-s, s) if s < 4 else (4,):
                    self.over(d, V)

        return event

    def finish(self):
        for d in (0, -1, 1, -2, 2, -3, 3, 4):
            self.over_got(d, V)


class ScatterKa:
    def __init__(self, net, Pn, Q, bufs, c):
        self.n, self.Pn, self.Q, self.c = net, Pn, Q, c
        self.x1a, self.x1b, self.y2, self.x2a, self.x2b, self.y1 = bufs
        self.k = KR[c]
        self.first, self.second = (0, self.k), (self.k, NR)

    def q(self, x, yl, lo, hi):
        return lambda: self.Q.at[(self.c,) + x + (slice(None) if yl is None else yl, pl.ds(lo, hi - lo))]

    def land(self, buf, rows, *where):
        return lambda: buf.at[(self.c,) + where + (pl.ds(0, rows[1] - rows[0]),)]

    def start(self):
        n, c = self.n, self.c
        n.send(lambda: self.Pn.at[c, :, :, :, n.cc1], lambda: self.Q.at[c], ("core", c), "cc")

    def far(self, buf, key, rows, yl):
        for d, sign, w in ways:
            part = halves(*rows)[d]
            if part[0] < part[1]:
                where = (d, slice(None)) if yl is None else (d,)
                self.n.send(self.q(self.n.xs[2], yl, *part), self.land(buf, part, *where), (key, self.c, d), "x" + w)

    def near(self, far, far_key, buf, key, rows, yl):
        for d, sign, w in ways:
            part = halves(*rows)[d]
            where = (d, slice(None)) if yl is None else (d,)
            if part[0] < part[1]:
                land = self.land(far, part, *where)
                self.n.recv(land, (far_key, self.c, d), "x" + w)
                accumulate(self.q(self.n.xs[sign], yl, *part)(), land())
            self.n.send(self.q(self.n.xs[sign], yl, *rows), self.land(buf, rows, *where), (key, self.c, d), "x" + w)

    def last(self, buf, key, rows, yl):
        for d, sign, w in ways:
            land = self.land(buf, rows, *((d, slice(None)) if yl is None else (d,)))
            self.n.recv(land, (key, self.c, d), "x" + w)
            accumulate(self.q(self.n.xs[0], yl, *rows)(), land())

    def one(self):
        n, c = self.n, self.c
        n.recv(lambda: self.Q.at[c], ("core", c), "cc")
        accumulate(self.Q.at[c], self.Pn.at[c, :, :, :, n.cc])
        if self.k < NR:
            src = lambda: self.Q.at[c, :, :, n.yl1, pl.ds(self.k, NR - self.k)]
            n.send(src, self.land(self.y2, self.second, slice(None), slice(None)), ("y2", c), "yl")
        self.far(self.x1a, "x1a", self.first, None)

    def two(self):
        self.near(self.x1a, "x1a", self.x1b, "x1b", self.first, None)

    def three(self):
        n, c = self.n, self.c
        if self.k < NR:
            land = self.land(self.y2, self.second, slice(None), slice(None))
            n.recv(land, ("y2", c), "yl")
            accumulate(self.Q.at[c, :, :, n.yl, pl.ds(self.k, NR - self.k)], land())
            self.far(self.x2a, "x2a", self.second, n.yl)

    def four(self):
        n, c = self.n, self.c
        self.last(self.x1b, "x1b", self.first, None)
        n.send(self.q(n.xs[0], n.yl1, *self.first), self.land(self.y1, self.first), ("y1", c), "yl")

    def five(self):
        if self.k < NR:
            self.near(self.x2a, "x2a", self.x2b, "x2b", self.second, self.n.yl)

    def six(self):
        n, c = self.n, self.c
        n.recv(self.land(self.y1, self.first), ("y1", c), "yl")
        accumulate(self.q(n.xs[0], n.yl, *self.first)(), self.land(self.y1, self.first)())
        if self.k < NR:
            self.last(self.x2b, "x2b", self.second, n.yl)


class GatherKa:
    def __init__(self, net, G, c):
        self.n, self.G, self.c = net, G, c
        self.k = KG[c]
        self.first, self.second = (0, self.k), (self.k, NR)
        self.mixed = self.k < NR

    def g(self, x, yl, core, lo, hi):
        return lambda: self.G.at[(self.c,) + x + (yl, core, pl.ds(lo, hi - lo))]

    def put(self, key, way, x, yl, rows):
        if rows[0] < rows[1]:
            ref = self.g(x, yl, self.n.cc, *rows)
            self.n.send(ref, ref, ("gk", self.c) + key, way)

    def get(self, key, way, x, yl, rows, other=False):
        if rows[0] < rows[1]:
            self.n.recv(self.g(x, yl, self.n.cc1 if other else self.n.cc, *rows), ("gk", self.c) + key, way)

    def zero(self):
        n = self.n
        self.put(("y1",), "yl", n.xs[0], n.yl, self.first)
        for d, sign, w in ways:
            self.put(("x2", d), "x" + w, n.xs[0], n.yl, (0, NR))
        self.put(("c0",), "cc", n.xs[0], n.yl, (0, NR))
        self.put(("y2", 0), "yl", n.xs[0], n.yl, self.second)

    def one(self):
        n = self.n
        self.get(("y1",), "yl", n.xs[0], n.yl1, self.first)
        for d, sign, w in ways:
            self.put(("x1", d), "x" + w, n.xs[0], n.yl1, self.first)
        self.put(("c1",), "cc", n.xs[0], n.yl1, self.first)

    def two(self):
        n = self.n
        for d, sign, w in ways:
            src = n.xs[-sign]
            self.get(("x2", d), "x" + w, src, n.yl, (0, NR))
            self.put(("x2h", d), "x" + w, src, n.yl, halves(0, NR)[d])
            self.put(("y2", 1 + d), "yl", src, n.yl, self.second)
            self.put(("c2", d), "cc", src, n.yl, (0, NR))

    def three(self):
        n = self.n
        for d, sign, w in ways:
            src = n.xs[-sign]
            self.get(("x1", d), "x" + w, src, n.yl1, self.first)
            self.put(("x1h", d), "x" + w, src, n.yl1, halves(*self.first)[d])
            self.put(("c3", d), "cc", src, n.yl1, self.first)

    def four(self):
        n = self.n
        for d, sign, w in ways:
            self.get(("x2h", d), "x" + w, n.xs[2], n.yl, halves(0, NR)[d])
        self.put(("y2", 3), "yl", n.xs[2], n.yl, self.second)
        self.put(("c4",), "cc", n.xs[2], n.yl, (0, NR))

    def five(self):
        n = self.n
        for d, sign, w in ways:
            self.get(("x1h", d), "x" + w, n.xs[2], n.yl1, halves(*self.first)[d])
        self.put(("c5",), "cc", n.xs[2], n.yl1, self.first)

    def six(self):
        n = self.n
        for k, x in enumerate((n.xs[0], n.xs[-1], n.xs[1], n.xs[2])):
            self.get(("y2", k), "yl", x, n.yl1, self.second)
            self.put(("c6", k), "cc", x, n.yl1, self.second)

    def finish(self):
        n = self.n
        self.get(("c0",), "cc", n.xs[0], n.yl, (0, NR), True)
        self.get(("c1",), "cc", n.xs[0], n.yl1, self.first, True)
        for d, sign, w in ways:
            src = n.xs[-sign]
            self.get(("c2", d), "cc", src, n.yl, (0, NR), True)
            self.get(("c3", d), "cc", src, n.yl1, self.first, True)
        self.get(("c4",), "cc", n.xs[2], n.yl, (0, NR), True)
        self.get(("c5",), "cc", n.xs[2], n.yl1, self.first, True)
        for k, x in enumerate((n.xs[0], n.xs[-1], n.xs[1], n.xs[2])):
            self.get(("c6", k), "cc", x, n.yl1, self.second, True)


class ScatterJa:
    def __init__(self, net, N, bufs, c):
        self.n, self.N, self.c = net, N, c
        self.ry, self.first, self.rest, self.rf = bufs

    def block(self, stream, z, lo, hi):
        col = self.n.yh1 if stream == "a" else self.n.yh
        return lambda: self.N.at[(self.c, col) + z + (pl.ds(lo, hi - lo),)]

    def land(self, stream, d, s):
        k = "uva".index(stream)
        if s == 1:
            return lambda: self.first.at[self.c, k, d]
        return lambda: self.rest.at[self.c, k, d, s - 2]

    def push(self, stream, s):
        for d, sign, w in ways:
            src = self.block(stream, self.n.zs[sign * (5 - s)], *rows_of(stream, d, s == 1))
            self.n.send(src, self.land(stream, d, s), ("rs", self.c, stream, d, s), "z" + w)

    def over(self, d):
        n, c = self.n, self.c
        src = lambda: self.N.at[(c, n.yh1) + n.zs[d] + (pl.ds(HR, HR),)]
        n.send(src, lambda: self.ry.at[c, d + 3], ("rsy", c, d), "yh")

    def over_got(self, d):
        n, c = self.n, self.c
        n.recv(lambda: self.ry.at[c, d + 3], ("rsy", c, d), "yh")
        accumulate(self.block("v", n.zs[d], *V)(), self.ry.at[c, d + 3])

    def start(self):
        self.over(4)
        self.push("a", 1)
        self.push("u", 1)
        for d in (3, -3, 2, -2, 1, -1, 0):
            self.over(d)

    def start_v(self):
        self.over_got(4)
        self.push("v", 1)

    def step(self, stream, s):
        def event():
            for d, sign, w in ways:
                if stream == "v" and (s < 4 or d == 0):
                    self.over_got(sign * (4 - s))
                land = self.land(stream, d, s)
                self.n.recv(land, ("rs", self.c, stream, d, s), "z" + w)
                accumulate(self.block(stream, self.n.zs[sign * (4 - s)], *rows_of(stream, d, s == 1))(), land())
            if s < 4:
                self.push(stream, s + 1)
            elif stream == "a":
                src = self.block("a", self.n.zs[0], *U)
                self.n.send(src, lambda: self.rf.at[self.c], ("rsf", self.c), "yh")

        return event

    def finish(self):
        n, c = self.n, self.c
        n.recv(lambda: self.rf.at[c], ("rsf", c), "yh")
        accumulate(self.block("u", n.zs[0], *U)(), self.rf.at[c])


def events_of(net, W, Pn, Q, ka_bufs, G, N, ja_bufs):
    table = {}
    for c in range(C):
        ag, rk = GatherJa(net, W, c), ScatterKa(net, Pn, Q, ka_bufs, c)
        gk, rj = GatherKa(net, G, c), ScatterJa(net, N, ja_bufs, c)
        table[f"ag{c}.start"] = ag.start
        table[f"ag{c}.start_a"] = ag.start_a
        for s in range(1, 5):
            for stream in streams:
                table[f"ag{c}.{stream}{s}"] = ag.step(stream, s)
                table[f"rj{c}.{stream}{s}"] = rj.step(stream, s)
        table[f"ag{c}.finish"] = ag.finish
        for name in ("start", "one", "two", "three", "four", "five", "six"):
            table[f"rk{c}.{name}"] = getattr(rk, name)
        for name in ("zero", "one", "two", "three", "four", "five", "six", "finish"):
            table[f"gk{c}.{name}"] = getattr(gk, name)
        for name in ("start", "start_v", "finish"):
            table[f"rj{c}.{name}"] = getattr(rj, name)
    return table


ORDER = (
    "prepare_left", "left0", "entered", "ag0.start", "left1", "prepare_right", "loaded",
    ("right", (3, "ag0.u1"), (3, "ag0.start_a"), (5, "ag0.v1"), (8, "ag0.u2"), (11, "ag0.a1"), (13, "ag0.v2"), (16, "ag0.u3"), (19, "ag0.a2"), (21, "ag0.v3"), (23, "ag0.u4"), (23, "ag1.start")),
    "ag0.a3", "ag0.v4", "ag1.u1", "ag1.v1", "ag1.start_a", "ag0.a4", "ag1.u2", "ag0.finish",
    ("turn_left0", (1, "ag1.v2"), (7, "ag1.a1")), "sent_left0",
    ("product0", (4, "ag1.u3"), (9, "ag1.v3"), (13, "ag1.a2")),
    ("turn_product0", (1, "ag1.u4"), (3, "ag1.v4"), (6, "ag1.a3")), "rk0.start", "ag1.a4", "ag1.finish",
    ("turn_left1", (7, "rk0.one"), (7, "sent_product0")), "sent_left1", ("product1", (10, "rk0.two")),
    ("turn_product1", (1, "rk0.three"), (6, "rk0.four")), "rk1.start", "rk0.five", "rk1.one", "sent_product1",
    "rk0.six", "rows0", "gk0.zero", "rk1.two", "gk0.two", "rk1.three", "rk1.four", "gk0.one", "gk0.four", "rk1.five",
    "gk0.three", "rk1.six", "rows1", "gk1.zero", "gk0.five", "gk0.six", "gk0.finish",
    ("turn_grad0", (3, "gk1.one"), (5, "gk1.two")),
    ("left_product0", (5, "gk1.three"), (9, "gk1.four"), (13, "gk1.five")), ("turn_back0", (4, "gk1.six")),
    "rj0.start", "gk1.finish", ("turn_grad1", (7, "rj0.a1")),
    ("left_product1", (1, "rj0.start_v"), (1, "rj0.u1"), (8, "rj0.a2"), (12, "rj0.v1"), (14, "rj0.u2")),
    ("turn_back1", (3, "rj0.a3"), (7, "rj0.v2")), "rj1.start", "rj0.u3",
    ("right_product", (3, "rj0.a4"), (6, "rj1.start_v"), (6, "rj0.v3"), (8, "rj1.a1"), (9, "rj1.u1"), (11, "rj0.u4"), (14, "rj1.v1")),
    "rj0.v4",
    ("right_pull", (2, "rj1.a2"), (3, "rj1.u2"), (5, "rj1.v2"), (6, "rj1.a3"), (6, "save0"), (7, "rj0.finish"), (7, "left_pull0"), (7, "rj1.u3"), (8, "rj1.v3"), (10, "rj1.a4"), (11, "rj1.u4"), (12, "save1"), (13, "rj1.v4"), (14, "rj1.finish"), (18, "save2")),
    "save3", "left_pull1",
)


def kernel(
    pair, slab, gain, left_gate, left_value, right_gate, right_value, out_gain, out_weight, cot,
    update, grad_pair, grad_slab,
    xv, wl_up, wl_low, wlc_hi, wlc_lo, wr_up, wr_low, wrc_hi, wrc_lo,
    W, Rt, Lt, Gt, Hb, N, Q, x1a, x1b, y2, x2a, x2b, y1, ry, first, rest, rf, ss, rs, local,
):
    net = Net(ss, rs)
    entered = net.greet()
    load = pltpu.make_async_copy(pair, xv, local.at[0])
    load.start()
    G, Pn = W, N
    events = events_of(net, W, Pn, Q, (x1a, x1b, y2, x2a, x2b, y1), G, N, (ry, first, rest, rf))

    Wf = W.reshape(C * 16 * NR, B, 128)
    Nf = N.reshape(C * 16 * NR, B, 128)
    flat_R = Rt.reshape(128 * B, 128)
    flat_H = Hb.reshape(128 * 128, 128)
    K = 4

    def right(t):
        made = forward(xv[pl.ds(t * K, K)].reshape(K * B, 128), wr_up, wr_low)
        for u in range(K):
            tile = jnp.concatenate([made[u * B : (u + 1) * B], jnp.zeros((32, 128), f32)], 0).T
            flat_R[pl.ds(t * K + u, 128, stride=B), :] = tile

    def each_h(make):
        def body(t):
            repeat(8, lambda u: make(t * 8 + u))

        return body

    def product(c):
        def make(h):
            Hb[h, c * CI : (c + 1) * CI, :B] = dot3(Lt[h, c * CI : (c + 1) * CI, :], Rt[h], NT)

        return each_h(make)

    def left_product(c):
        def make(h):
            turned = jnp.concatenate([Rt[h], jnp.zeros((32, 128), f32)], 0)
            Hb[h, c * CI : (c + 1) * CI, :] = dot3(Gt[h, c * CI : (c + 1) * CI, :], turned)

        return each_h(make)

    def right_product(h):
        Hb[h, :B, :] = dot3(Gt[h].T, Lt[h])[:B]

    def right_pull(t):
        grads = [flat_H[pl.ds(t * K + u, 128, stride=128), :].T[:B] for u in range(K)]
        rows = xv[pl.ds(t * K, K)].reshape(K * B, 128)
        out = pull(rows, jnp.concatenate(grads, 0), wr_up, wr_low, wrc_hi, wrc_lo)
        xv[pl.ds(t * K, K)] = out.reshape(K, B, 128)

    loops = {
        "right": (B // K, right),
        "right_product": (16, each_h(right_product)),
        "right_pull": (B // K, right_pull),
    }

    def turn_in(dst, c):
        return lambda t: rows_in(Wf, dst, c * CI + t * 8, 8)

    def turn_out(c):
        return lambda t: rows_out(Hb, Nf, c * CI + t * 8, 8)

    for c in range(C):
        loops[f"turn_left{c}"] = (CI // 8, turn_in(Lt, c))
        loops[f"product{c}"] = (16, product(c))
        loops[f"turn_product{c}"] = (CI // 8, turn_out(c))
        loops[f"turn_grad{c}"] = (CI // 8, turn_in(Gt, c))
        loops[f"left_product{c}"] = (16, left_product(c))
        loops[f"turn_back{c}"] = (CI // 8, turn_out(c))

    def left(c):
        def step():
            own = forward(slab[c * NR : (c + 1) * NR].reshape(NR * B, 128), wl_up, wl_low)
            W[(c, net.yh) + net.zs[0]] = own.reshape(NR, B, 128)

        return step

    def rows(c):
        def step():
            mine = (c,) + net.xs[0] + (net.yl,)

            def one(u):
                r = c * NR + u
                normed, scale = normalise(Q[mine + (u,)])
                update[r] = dot3(normed * out_gain[...], out_weight[...])
                d = dot3(cot[r], out_weight[...], NT) * out_gain[...]
                G[mine + (net.cc, u)] = scale * (d - mean(d) - normed * mean(d * normed))

            repeat(NR, one)

        return step

    def left_pull(c):
        def step():
            grads = N[(c, net.yh) + net.zs[0]].reshape(NR * B, 128)
            out = pull(slab[c * NR : (c + 1) * NR].reshape(NR * B, 128), grads, wl_up, wl_low, wlc_hi, wlc_lo)
            grad_slab[c * NR : (c + 1) * NR] = out.reshape(NR, B, 128)

        return step

    def save(k):
        part = pl.ds(k * (B // 4), B // 4)
        return pltpu.make_async_copy(xv.at[part], grad_pair.at[part], local.at[1 + k])

    steps = {
        "prepare_left": lambda: prepare(gain, left_gate, left_value, wl_up, wl_low, wlc_hi, wlc_lo),
        "prepare_right": lambda: prepare(gain, right_gate, right_value, wr_up, wr_low, wrc_hi, wrc_lo),
        "entered": entered,
        "loaded": load.wait,
    }
    for k in range(4):
        steps[f"save{k}"] = lambda k=k: save(k).start()
    for c in range(C):
        steps[f"left{c}"] = left(c)
        steps[f"rows{c}"] = rows(c)
        steps[f"left_pull{c}"] = left_pull(c)
        steps[f"sent_left{c}"] = lambda c=c: net.drain(("ag", c), ("agy", c))
        steps[f"sent_product{c}"] = lambda c=c: net.drain(("core", c))
    steps.update(events)

    for entry in ORDER:
        if isinstance(entry, str):
            steps[entry]()
        else:
            run(*loops[entry[0]], [(t, steps[name]) for t, name in entry[1:]])
    net.drain()
    for k in range(4):
        save(k).wait()


def shards(
    pair_map, slab_rows, norm_gain, left_gate, left_value, right_gate, right_value, out_gain, out_weight, cotangent
):
    S = jax.ShapeDtypeStruct
    M = pltpu.VMEM
    weights = [M((256, 256), bf16)] + [M((128, 256), bf16)] * 3
    return pl.pallas_call(
        kernel,
        out_shape=[S((8,) + T, f32), S((B,) + T, f32), S((8,) + T, f32)],
        in_specs=[HBM] + [VM] * 9,
        out_specs=[VM, HBM, VM],
        scratch_shapes=[M((B,) + T, f32)]
        + weights * 2
        + [
            M((C, 2, 2, 2, 2, NR) + T, f32),
            M((128, B, 128), f32),
            M((128, 128, 128), f32),
            M((128, 128, 128), f32),
            M((128, 128, 128), f32),
            M((C, 2, 2, 2, 2, NR) + T, f32),
            M((C, 2, 2, 2, NR) + T, f32),
            M((C, 2, YL, UP(max(KR))) + T, f32),
            M((C, 2, YL, max(KR)) + T, f32),
            M((C, 2, 2, max(NR - min(KR), 1)) + T, f32),
            M((C, 2, max(UP(NR - min(KR)), 1)) + T, f32),
            M((C, 2, max(NR - min(KR), 1)) + T, f32),
            M((C, max(KR)) + T, f32),
            M((C, Z, HR) + T, f32),
            M((C, 3, 2, QR) + T, f32),
            M((C, 3, 2, 3, HR) + T, f32),
            M((C, HR) + T, f32),
            pltpu.SemaphoreType.DMA((240,)),
            pltpu.SemaphoreType.DMA((240,)),
            pltpu.SemaphoreType.DMA((5,)),
        ],
        compiler_params=pltpu.CompilerParams(collective_id=1, has_side_effects=True, vmem_limit_bytes=63 * MIB),
        name="triangle",
    )(
        pair_map, slab_rows, norm_gain.reshape(1, 128), left_gate, left_value, right_gate, right_value,
        out_gain.reshape(1, 128), out_weight, cotangent,
    )


def solution(mesh):
    in_specs = (
        P("ja", "ka", None),
        P("ja", "ka", None),
        P(),
        P(),
        P(),
        P(),
        P(),
        P(),
        P(),
        P("ka", "ja", None),
    )
    out_specs = (P("ka", "ja", None), P("ja", "ka", None), P("ja", "ka", None))
    return jax.shard_map(shards, mesh=mesh, in_specs=in_specs, out_specs=out_specs, check_vma=False)
```

time: 574 us -> 197 us (0.34)
  waiting for transfers between devices: 371 us -> 0 us
  Pallas kernels: 0 us -> 188 us
  matrix products: 108 us -> 0 us
  local copies, waits for them, and re-layouts: 43.8 us -> 7.41 us
  other arithmetic: 32.1 us -> 0 us
  between operations: 14.4 us -> 0.64 us
    reduce_scatter x2 -> x0, waiting for transfers between devices: 237 us -> none  [the longest x1 164 us: shards(): lax.psum_scatter(jnp.einsum('ijh,jkh->ikh', picked, right_map, precision=...]
    pallas_call x0 -> x1, Pallas kernels: none -> 188 us  [shards(): pl.pallas_call(kernel, out_shape=[S((8,) + T, f32), S((B,) + T, f32), S((...]
    all_gather x2 -> x0, waiting for transfers between devices: 133 us -> none  [the longest x1 85.2 us: shards(): whole_left = lax.all_gather(left_local, 'ja', axis=0, tiled=True)]
    dot_general x13 -> x0, matrix products: 108 us -> none  [the longest x1 22.5 us: shards(): jnp.einsum('ikh,jkh->ijh', picked, right_map, precision=lax.Precision.HIG...]
    reduce_sum x8 -> x0, other arithmetic: 21.9 us -> none  [the longest x6 14.9 us: layer_norm(): center = values - jnp.mean(values, axis=-1, keepdims=True)]
    all_gather x2 -> x0, local copies, waits for them, and re-layouts: 16.8 us -> none  [the longest x1 8.43 us: shards(): whole_left = lax.all_gather(left_local, 'ja', axis=0, tiled=True)]
    dot_general x2 -> x0, local copies, waits for them, and re-layouts: 12.9 us -> none  [the longest x1 6.67 us: shards(): jnp.einsum('ijh,jkh->ikh', picked, right_map, precision=lax.Precision.HIG...]
    add_any x3 -> x0, other arithmetic: 10.1 us -> none  [layer_norm(): center = values - jnp.mean(values, axis=-1, keepdims=True)]
  transfers between devices with their start and end apart: 4 -> 0, of which waited for: 4 -> 0; matrix products, arithmetic and copies ran while one was open for 16% -> 0% of each run, Pallas kernels for 0% -> 0%
where the time goes in v2:
time: 197 us; the launch traced here: 196 us
  Pallas kernels  188 us (95%)
  local copies, waits for them, and re-layouts  7.41 us (4%)
    pallas_call x1, Pallas kernels, shards(): pl.pallas_call(kernel, out_shape=[S((8,) + T, f32), S((B,) + T, f32), S((...  188 us
    unnamed x5, local copies, waits for them, and re-layouts  7.41 us

profile of v2, /device:TPU:2, one launch (start us, length us, event | category | flops | bytes accessed | tf_op | source)
XLA Modules:
  0.0 196.2 jit_solution(13977165612007505841)
XLA Ops:
  0.6 188.2 %triangle.1 = (f32[8,96,128]{2,1,0:T(8,128)}, f32[96,96,128]{2,1,0:T(8,128)}, f32[8,96,128]{2,1,0:T(8,128)}) custom-call(f32[96,96,128]{2,1,0:T(8,128)} %pair.1, f32[8,96,128]{2,1,0:T(8,128)} %slab.1, f32[1,128]{1,0:T(1,128)} %bitcast.2, f32[128,128]{1,0:T(8,128)} %left_gate.1, f32[128,128]{1,0:T(8,128)} %left_value.1, f32[128,128]{1,0:T(8,128)} %right_gate.1, ...), custom_call_target="tpu_custom_call" | custom-call | tf_op jit(solution)/shard_map/triangle/pallas_call | solution.py:676
  188.8 1.8 copy.16
  190.6 0.0 copy-start
  190.6 4.9 %copy.17 = f32[96,96,128]{2,1,0:T(8,128)} copy(f32[96,96,128]{2,1,0:T(8,128)} %get-tuple-element.7) | data formatting | bytes 9437184
  195.5 0.0 copy-done
  195.5 0.7 copy.18
Async XLA Ops:
  190.6 4.9 %copy-start = (f32[8,96,128]{2,1,0:T(8,128)S(1)}, f32[8,96,128]{2,1,0:T(8,128)}, u32[]{:S(2)}) copy-start(f32[8,96,128]{2,1,0:T(8,128)} %get-tuple-element.8) | copy-start | bytes 1179652

commit v3 on v2

--- a/solution.py
+++ b/solution.py
@@ -1,3 +1,5 @@
+from types import SimpleNamespace
+
 import jax
 import jax.numpy as jnp
 from jax import lax
@@ -16,6 +18,7 @@
 KG = (2, 2)
 CI = 16 * NR
 B = 96
+HS = 136
 T = (B, 128)
 MIB = 2**20
 MESH = pl.DeviceIdType.MESH
@@ -39,6 +42,15 @@
     b_hi, b_lo = split(b)
     both = dot(jnp.concatenate([a_hi, a_lo], 1), jnp.concatenate([b_hi, b_hi], dims[0][1][0]), dims)
     return both + dot(a_hi, b_lo, dims)
+
+
+def dot3_wide(a, b):
+    a_hi, a_lo = split(a)
+    b_hi, b_lo = split(b)
+    upper = jnp.concatenate([b_hi, b_lo], 1)
+    lower = jnp.concatenate([b_hi, jnp.zeros_like(b_lo)], 1)
+    both = dot(jnp.concatenate([a_hi, a_lo], 1), jnp.concatenate([upper, lower], 0))
+    return both[:, : b.shape[1]] + both[:, b.shape[1] :]
 
 
 def mean(values):
@@ -219,6 +231,7 @@
 class GatherJa:
     def __init__(self, net, W, c):
         self.n, self.W, self.c = net, W, c
+        self.u, self.v, self.a = [{s: self.step(k, s) for s in range(1, 5)} for k in streams]
 
     def at(self, yh, z, lo, hi):
         return lambda: self.W.at[(self.c, yh) + z + (pl.ds(lo, hi - lo),)]
@@ -431,6 +444,7 @@
     def __init__(self, net, N, bufs, c):
         self.n, self.N, self.c = net, N, c
         self.ry, self.first, self.rest, self.rf = bufs
+        self.u, self.v, self.a = [{s: self.step(k, s) for s in range(1, 5)} for k in streams]
 
     def block(self, stream, z, lo, hi):
         col = self.n.yh1 if stream == "a" else self.n.yh
@@ -490,48 +504,28 @@
         accumulate(self.block("u", n.zs[0], *U)(), self.rf.at[c])
 
 
-def events_of(net, W, Pn, Q, ka_bufs, G, N, ja_bufs):
-    table = {}
-    for c in range(C):
-        ag, rk = GatherJa(net, W, c), ScatterKa(net, Pn, Q, ka_bufs, c)
-        gk, rj = GatherKa(net, G, c), ScatterJa(net, N, ja_bufs, c)
-        table[f"ag{c}.start"] = ag.start
-        table[f"ag{c}.start_a"] = ag.start_a
-        for s in range(1, 5):
-            for stream in streams:
-                table[f"ag{c}.{stream}{s}"] = ag.step(stream, s)
-                table[f"rj{c}.{stream}{s}"] = rj.step(stream, s)
-        table[f"ag{c}.finish"] = ag.finish
-        for name in ("start", "one", "two", "three", "four", "five", "six"):
-            table[f"rk{c}.{name}"] = getattr(rk, name)
-        for name in ("zero", "one", "two", "three", "four", "five", "six", "finish"):
-            table[f"gk{c}.{name}"] = getattr(gk, name)
-        for name in ("start", "start_v", "finish"):
-            table[f"rj{c}.{name}"] = getattr(rj, name)
-    return table
-
-
-ORDER = (
-    "prepare_left", "left0", "entered", "ag0.start", "left1", "prepare_right", "loaded",
-    ("right", (3, "ag0.u1"), (3, "ag0.start_a"), (5, "ag0.v1"), (8, "ag0.u2"), (11, "ag0.a1"), (13, "ag0.v2"), (16, "ag0.u3"), (19, "ag0.a2"), (21, "ag0.v3"), (23, "ag0.u4"), (23, "ag1.start")),
-    "ag0.a3", "ag0.v4", "ag1.u1", "ag1.v1", "ag1.start_a", "ag0.a4", "ag1.u2", "ag0.finish",
-    ("turn_left0", (1, "ag1.v2"), (7, "ag1.a1")), "sent_left0",
-    ("product0", (4, "ag1.u3"), (9, "ag1.v3"), (13, "ag1.a2")),
-    ("turn_product0", (1, "ag1.u4"), (3, "ag1.v4"), (6, "ag1.a3")), "rk0.start", "ag1.a4", "ag1.finish",
-    ("turn_left1", (7, "rk0.one"), (7, "sent_product0")), "sent_left1", ("product1", (10, "rk0.two")),
-    ("turn_product1", (1, "rk0.three"), (6, "rk0.four")), "rk1.start", "rk0.five", "rk1.one", "sent_product1",
-    "rk0.six", "rows0", "gk0.zero", "rk1.two", "gk0.two", "rk1.three", "rk1.four", "gk0.one", "gk0.four", "rk1.five",
-    "gk0.three", "rk1.six", "rows1", "gk1.zero", "gk0.five", "gk0.six", "gk0.finish",
-    ("turn_grad0", (3, "gk1.one"), (5, "gk1.two")),
-    ("left_product0", (5, "gk1.three"), (9, "gk1.four"), (13, "gk1.five")), ("turn_back0", (4, "gk1.six")),
-    "rj0.start", "gk1.finish", ("turn_grad1", (7, "rj0.a1")),
-    ("left_product1", (1, "rj0.start_v"), (1, "rj0.u1"), (8, "rj0.a2"), (12, "rj0.v1"), (14, "rj0.u2")),
-    ("turn_back1", (3, "rj0.a3"), (7, "rj0.v2")), "rj1.start", "rj0.u3",
-    ("right_product", (3, "rj0.a4"), (6, "rj1.start_v"), (6, "rj0.v3"), (8, "rj1.a1"), (9, "rj1.u1"), (11, "rj0.u4"), (14, "rj1.v1")),
-    "rj0.v4",
-    ("right_pull", (2, "rj1.a2"), (3, "rj1.u2"), (5, "rj1.v2"), (6, "rj1.a3"), (6, "save0"), (7, "rj0.finish"), (7, "left_pull0"), (7, "rj1.u3"), (8, "rj1.v3"), (10, "rj1.a4"), (11, "rj1.u4"), (12, "save1"), (13, "rj1.v4"), (14, "rj1.finish"), (18, "save2")),
-    "save3", "left_pull1",
-)
+def order(ag, rk, gk, rj, do, loop):
+    return (
+        do.prepare_left, do.left[0], do.entered, ag[0].start, do.left[1], do.prepare_right, do.loaded, (loop.right,
+        (2, ag[0].u[1]), (2, ag[0].start_a), (4, ag[0].v[1]), (5, ag[0].u[2]), (7, ag[0].a[1]), (9, ag[0].v[2]),
+        (11, ag[0].u[3])), ag[0].a[2], ag[0].v[3], ag[0].u[4], ag[1].start, ag[0].a[3], ag[0].v[4], ag[1].u[1],
+        ag[1].v[1], ag[1].start_a, ag[0].a[4], ag[1].u[2], ag[0].finish, (loop.turn_left[0], (1, ag[1].v[2]), (6,
+        ag[1].a[1])), do.sent_left[0], (loop.product[0], (2, ag[1].u[3]), (4, ag[1].v[3]), (5, ag[1].a[2]), (7,
+        ag[1].u[4])), ag[1].v[4], (loop.turn_product[0], (4, ag[1].a[3])), rk[0].start, ag[1].a[4], ag[1].finish,
+        (loop.turn_left[1], (7, rk[0].one), (7, do.sent_product[0])), do.sent_left[1], (loop.product[1], (4,
+        rk[0].two)), rk[0].three, (loop.turn_product[1], (3, rk[0].four)), rk[1].start, rk[0].five, rk[1].one,
+        do.sent_product[1], rk[0].six, do.rows[0], gk[0].zero, rk[1].two, gk[0].two, rk[1].three, rk[1].four,
+        gk[0].one, gk[0].four, rk[1].five, gk[0].three, rk[1].six, do.rows[1], gk[1].zero, gk[0].five, gk[0].six,
+        gk[0].finish, (loop.turn_grad[0], (3, gk[1].one), (4, gk[1].two)), (loop.left_product[0], (3, gk[1].three),
+        (5, gk[1].four)), gk[1].five, (loop.turn_back[0], (7, gk[1].six)), rj[0].start, gk[1].finish,
+        (loop.turn_grad[1], (6, rj[0].a[1]), (7, rj[0].start_v), (7, rj[0].u[1])), (loop.left_product[1], (4,
+        rj[0].a[2]), (6, rj[0].v[1])), rj[0].u[2], (loop.turn_back[1], (5, rj[0].a[3])), rj[1].start, rj[0].v[2],
+        (loop.right_product, (2, rj[0].u[3]), (6, rj[0].a[4]), (9, rj[1].a[1]), (9, rj[1].start_v), (10,
+        rj[1].u[1]), (12, rj[0].v[3])), rj[0].u[4], (loop.right_pull, (1, rj[1].a[2]), (2, rj[1].v[1]), (3,
+        rj[1].u[2]), (3, do.save[0]), (4, rj[0].v[4]), (5, rj[1].a[3]), (6, rj[1].v[2]), (6, rj[0].finish), (6,
+        do.left_pull[0]), (6, rj[1].u[3]), (6, do.save[1]), (7, rj[1].a[4]), (8, rj[1].v[3]), (9, rj[1].u[4]), (9,
+        do.save[2]), (11, rj[1].v[4]), (11, rj[1].finish)), do.save[3], do.left_pull[1],
+    )
 
 
 def kernel(
@@ -545,13 +539,17 @@
     load = pltpu.make_async_copy(pair, xv, local.at[0])
     load.start()
     G, Pn = W, N
-    events = events_of(net, W, Pn, Q, (x1a, x1b, y2, x2a, x2b, y1), G, N, (ry, first, rest, rf))
+    each = range(C)
+    ag = [GatherJa(net, W, c) for c in each]
+    rk = [ScatterKa(net, Pn, Q, (x1a, x1b, y2, x2a, x2b, y1), c) for c in each]
+    gk = [GatherKa(net, G, c) for c in each]
+    rj = [ScatterJa(net, N, (ry, first, rest, rf), c) for c in each]
 
     Wf = W.reshape(C * 16 * NR, B, 128)
     Nf = N.reshape(C * 16 * NR, B, 128)
     flat_R = Rt.reshape(128 * B, 128)
-    flat_H = Hb.reshape(128 * 128, 128)
-    K = 4
+    flat_H = Hb.reshape(128 * HS, 128)
+    K = 8
 
     def right(t):
         made = forward(xv[pl.ds(t * K, K)].reshape(K * B, 128), wr_up, wr_low)
@@ -559,53 +557,48 @@
             tile = jnp.concatenate([made[u * B : (u + 1) * B], jnp.zeros((32, 128), f32)], 0).T
             flat_R[pl.ds(t * K + u, 128, stride=B), :] = tile
 
-    def each_h(make):
-        def body(t):
-            repeat(8, lambda u: make(t * 8 + u))
-
-        return body
+    def each_h(n, make):
+        return 128 // n, lambda t: repeat(n, lambda u: make(t * n + u))
 
     def product(c):
         def make(h):
             Hb[h, c * CI : (c + 1) * CI, :B] = dot3(Lt[h, c * CI : (c + 1) * CI, :], Rt[h], NT)
 
-        return each_h(make)
+        return each_h(16, make)
 
     def left_product(c):
         def make(h):
             turned = jnp.concatenate([Rt[h], jnp.zeros((32, 128), f32)], 0)
-            Hb[h, c * CI : (c + 1) * CI, :] = dot3(Gt[h, c * CI : (c + 1) * CI, :], turned)
-
-        return each_h(make)
+            Hb[h, c * CI : (c + 1) * CI, :] = dot3_wide(Gt[h, c * CI : (c + 1) * CI, :], turned)
+
+        return each_h(16, make)
 
     def right_product(h):
-        Hb[h, :B, :] = dot3(Gt[h].T, Lt[h])[:B]
+        Hb[h, :B, :] = dot3_wide(Gt[h].T, Lt[h])[:B]
 
     def right_pull(t):
-        grads = [flat_H[pl.ds(t * K + u, 128, stride=128), :].T[:B] for u in range(K)]
+        grads = [flat_H[pl.ds(t * K + u, 128, stride=HS), :].T[:B] for u in range(K)]
         rows = xv[pl.ds(t * K, K)].reshape(K * B, 128)
         out = pull(rows, jnp.concatenate(grads, 0), wr_up, wr_low, wrc_hi, wrc_lo)
         xv[pl.ds(t * K, K)] = out.reshape(K, B, 128)
 
-    loops = {
-        "right": (B // K, right),
-        "right_product": (16, each_h(right_product)),
-        "right_pull": (B // K, right_pull),
-    }
-
     def turn_in(dst, c):
-        return lambda t: rows_in(Wf, dst, c * CI + t * 8, 8)
+        return CI // 8, lambda t: rows_in(Wf, dst, c * CI + t * 8, 8)
 
     def turn_out(c):
-        return lambda t: rows_out(Hb, Nf, c * CI + t * 8, 8)
-
-    for c in range(C):
-        loops[f"turn_left{c}"] = (CI // 8, turn_in(Lt, c))
-        loops[f"product{c}"] = (16, product(c))
-        loops[f"turn_product{c}"] = (CI // 8, turn_out(c))
-        loops[f"turn_grad{c}"] = (CI // 8, turn_in(Gt, c))
-        loops[f"left_product{c}"] = (16, left_product(c))
-        loops[f"turn_back{c}"] = (CI // 8, turn_out(c))
+        return CI // 8, lambda t: rows_out(Hb, Nf, c * CI + t * 8, 8)
+
+    loop = SimpleNamespace(
+        right=(B // K, right),
+        turn_left=[turn_in(Lt, c) for c in each],
+        product=[product(c) for c in each],
+        turn_product=[turn_out(c) for c in each],
+        turn_grad=[turn_in(Gt, c) for c in each],
+        left_product=[left_product(c) for c in each],
+        turn_back=[turn_out(c) for c in each],
+        right_product=each_h(8, right_product),
+        right_pull=(B // K, right_pull),
+    )
 
     def left(c):
         def step():
@@ -641,27 +634,25 @@
         part = pl.ds(k * (B // 4), B // 4)
         return pltpu.make_async_copy(xv.at[part], grad_pair.at[part], local.at[1 + k])
 
-    steps = {
-        "prepare_left": lambda: prepare(gain, left_gate, left_value, wl_up, wl_low, wlc_hi, wlc_lo),
-        "prepare_right": lambda: prepare(gain, right_gate, right_value, wr_up, wr_low, wrc_hi, wrc_lo),
-        "entered": entered,
-        "loaded": load.wait,
-    }
-    for k in range(4):
-        steps[f"save{k}"] = lambda k=k: save(k).start()
-    for c in range(C):
-        steps[f"left{c}"] = left(c)
-        steps[f"rows{c}"] = rows(c)
-        steps[f"left_pull{c}"] = left_pull(c)
-        steps[f"sent_left{c}"] = lambda c=c: net.drain(("ag", c), ("agy", c))
-        steps[f"sent_product{c}"] = lambda c=c: net.drain(("core", c))
-    steps.update(events)
-
-    for entry in ORDER:
-        if isinstance(entry, str):
-            steps[entry]()
+    do = SimpleNamespace(
+        prepare_left=lambda: prepare(gain, left_gate, left_value, wl_up, wl_low, wlc_hi, wlc_lo),
+        prepare_right=lambda: prepare(gain, right_gate, right_value, wr_up, wr_low, wrc_hi, wrc_lo),
+        entered=entered,
+        loaded=load.wait,
+        left=[left(c) for c in each],
+        rows=[rows(c) for c in each],
+        left_pull=[left_pull(c) for c in each],
+        save=[lambda k=k: save(k).start() for k in range(4)],
+        sent_left=[lambda c=c: net.drain(("ag", c), ("agy", c)) for c in each],
+        sent_product=[lambda c=c: net.drain(("core", c)) for c in each],
+    )
+
+    for entry in order(ag, rk, gk, rj, do, loop):
+        if isinstance(entry, tuple):
+            (n, body), *events = entry
+            run(n, body, events)
         else:
-            run(*loops[entry[0]], [(t, steps[name]) for t, name in entry[1:]])
+            entry()
     net.drain()
     for k in range(4):
         save(k).wait()
@@ -685,7 +676,7 @@
             M((128, B, 128), f32),
             M((128, 128, 128), f32),
             M((128, 128, 128), f32),
-            M((128, 128, 128), f32),
+            M((128, HS, 128), f32),
             M((C, 2, 2, 2, 2, NR) + T, f32),
             M((C, 2, 2, 2, NR) + T, f32),
             M((C, 2, YL, UP(max(KR))) + T, f32),

time: 197 us -> 182 us (0.924)
  Pallas kernels: 188 us -> 172 us
    pallas_call x1, Pallas kernels: 188 us -> 172 us  [shards(): pl.pallas_call(kernel, out_shape=[S((8,) + T, f32), S((B,) + T, f32), S((...]
where the time goes in v3:
time: 182 us; the launch traced here: 180 us
  Pallas kernels  172 us (95%)
  local copies, waits for them, and re-layouts  7.41 us (4%)
    pallas_call x1, Pallas kernels, shards(): pl.pallas_call(kernel, out_shape=[S((8,) + T, f32), S((B,) + T, f32), S((...  172 us
    unnamed x5, local copies, waits for them, and re-layouts  7.41 us

profile of v3, /device:TPU:2, one launch (start us, length us, event | category | flops | bytes accessed | tf_op | source)
XLA Modules:
  0.0 179.8 jit_solution(16734329794401282751)
XLA Ops:
  0.6 171.7 %triangle.1 = (f32[8,96,128]{2,1,0:T(8,128)}, f32[96,96,128]{2,1,0:T(8,128)}, f32[8,96,128]{2,1,0:T(8,128)}) custom-call(f32[96,96,128]{2,1,0:T(8,128)} %pair.1, f32[8,96,128]{2,1,0:T(8,128)} %slab.1, f32[1,128]{1,0:T(1,128)} %bitcast.2, f32[128,128]{1,0:T(8,128)} %left_gate.1, f32[128,128]{1,0:T(8,128)} %left_value.1, f32[128,128]{1,0:T(8,128)} %right_gate.1, ...), custom_call_target="tpu_custom_call" | custom-call | tf_op jit(solution)/shard_map/triangle/pallas_call | solution.py:667
  172.4 1.8 copy.16
  174.1 0.0 copy-start
  174.1 4.9 %copy.17 = f32[96,96,128]{2,1,0:T(8,128)} copy(f32[96,96,128]{2,1,0:T(8,128)} %get-tuple-element.7) | data formatting | bytes 9437184
  179.0 0.0 copy-done
  179.0 0.7 copy.18
Async XLA Ops:
  174.1 4.9 %copy-start = (f32[8,96,128]{2,1,0:T(8,128)S(1)}, f32[8,96,128]{2,1,0:T(8,128)}, u32[]{:S(2)}) copy-start(f32[8,96,128]{2,1,0:T(8,128)} %get-tuple-element.8) | copy-start | bytes 1179652

commit v4 on v3

--- a/solution.py
+++ b/solution.py
@@ -86,9 +86,8 @@
     return s * v
 
 
-def pull(values, grad, w_up, w_low, wc_hi, wc_lo):
+def pull(values, grad, s, v, wc_hi, wc_lo):
     normed, scale = normalise(values)
-    s, v = gates(normed, w_up, w_low)
     d_value = grad * s
     d_gate = d_value * v * (1.0 - s)
     hi, lo = split(jnp.concatenate([d_gate, d_value], 1))
@@ -292,9 +291,15 @@
     def land(self, buf, rows, *where):
         return lambda: buf.at[(self.c,) + where + (pl.ds(0, rows[1] - rows[0]),)]
 
+    def halves_of_core(self):
+        return [rows for rows in (self.second, self.first) if rows[0] < rows[1]]
+
     def start(self):
         n, c = self.n, self.c
-        n.send(lambda: self.Pn.at[c, :, :, :, n.cc1], lambda: self.Q.at[c], ("core", c), "cc")
+        for k, (lo, hi) in enumerate(self.halves_of_core()):
+            part = pl.ds(lo, hi - lo)
+            src = lambda part=part: self.Pn.at[c, :, :, :, n.cc1, part]
+            n.send(src, lambda part=part: self.Q.at[c, :, :, :, part], ("core", c, k), "cc")
 
     def far(self, buf, key, rows, yl):
         for d, sign, w in ways:
@@ -321,11 +326,13 @@
 
     def one(self):
         n, c = self.n, self.c
-        n.recv(lambda: self.Q.at[c], ("core", c), "cc")
-        accumulate(self.Q.at[c], self.Pn.at[c, :, :, :, n.cc])
-        if self.k < NR:
-            src = lambda: self.Q.at[c, :, :, n.yl1, pl.ds(self.k, NR - self.k)]
-            n.send(src, self.land(self.y2, self.second, slice(None), slice(None)), ("y2", c), "yl")
+        for k, (lo, hi) in enumerate(self.halves_of_core()):
+            part = pl.ds(lo, hi - lo)
+            n.recv(lambda: self.Q.at[c, :, :, :, part], ("core", c, k), "cc")
+            accumulate(self.Q.at[c, :, :, :, part], self.Pn.at[c, :, :, :, n.cc, part])
+            if lo > 0:
+                land = self.land(self.y2, self.second, slice(None), slice(None))
+                n.send(lambda part=part: self.Q.at[c, :, :, n.yl1, part], land, ("y2", c), "yl")
         self.far(self.x1a, "x1a", self.first, None)
 
     def two(self):
@@ -507,30 +514,31 @@
 def order(ag, rk, gk, rj, do, loop):
     return (
         do.prepare_left, do.left[0], do.entered, ag[0].start, do.left[1], do.prepare_right, do.loaded, (loop.right,
-        (2, ag[0].u[1]), (2, ag[0].start_a), (4, ag[0].v[1]), (5, ag[0].u[2]), (7, ag[0].a[1]), (9, ag[0].v[2]),
-        (11, ag[0].u[3])), ag[0].a[2], ag[0].v[3], ag[0].u[4], ag[1].start, ag[0].a[3], ag[0].v[4], ag[1].u[1],
-        ag[1].v[1], ag[1].start_a, ag[0].a[4], ag[1].u[2], ag[0].finish, (loop.turn_left[0], (1, ag[1].v[2]), (6,
-        ag[1].a[1])), do.sent_left[0], (loop.product[0], (2, ag[1].u[3]), (4, ag[1].v[3]), (5, ag[1].a[2]), (7,
-        ag[1].u[4])), ag[1].v[4], (loop.turn_product[0], (4, ag[1].a[3])), rk[0].start, ag[1].a[4], ag[1].finish,
-        (loop.turn_left[1], (7, rk[0].one), (7, do.sent_product[0])), do.sent_left[1], (loop.product[1], (4,
-        rk[0].two)), rk[0].three, (loop.turn_product[1], (3, rk[0].four)), rk[1].start, rk[0].five, rk[1].one,
-        do.sent_product[1], rk[0].six, do.rows[0], gk[0].zero, rk[1].two, gk[0].two, rk[1].three, rk[1].four,
-        gk[0].one, gk[0].four, rk[1].five, gk[0].three, rk[1].six, do.rows[1], gk[1].zero, gk[0].five, gk[0].six,
-        gk[0].finish, (loop.turn_grad[0], (3, gk[1].one), (4, gk[1].two)), (loop.left_product[0], (3, gk[1].three),
-        (5, gk[1].four)), gk[1].five, (loop.turn_back[0], (7, gk[1].six)), rj[0].start, gk[1].finish,
-        (loop.turn_grad[1], (6, rj[0].a[1]), (7, rj[0].start_v), (7, rj[0].u[1])), (loop.left_product[1], (4,
-        rj[0].a[2]), (6, rj[0].v[1])), rj[0].u[2], (loop.turn_back[1], (5, rj[0].a[3])), rj[1].start, rj[0].v[2],
-        (loop.right_product, (2, rj[0].u[3]), (6, rj[0].a[4]), (9, rj[1].a[1]), (9, rj[1].start_v), (10,
-        rj[1].u[1]), (12, rj[0].v[3])), rj[0].u[4], (loop.right_pull, (1, rj[1].a[2]), (2, rj[1].v[1]), (3,
-        rj[1].u[2]), (3, do.save[0]), (4, rj[0].v[4]), (5, rj[1].a[3]), (6, rj[1].v[2]), (6, rj[0].finish), (6,
-        do.left_pull[0]), (6, rj[1].u[3]), (6, do.save[1]), (7, rj[1].a[4]), (8, rj[1].v[3]), (9, rj[1].u[4]), (9,
-        do.save[2]), (11, rj[1].v[4]), (11, rj[1].finish)), do.save[3], do.left_pull[1],
+        (2, ag[0].u[1]), (2, ag[0].start_a), (3, ag[0].v[1]), (5, ag[0].u[2]), (7, ag[0].a[1]), (9, ag[0].v[2]),
+        (10, ag[0].u[3])), ag[0].a[2], do.keep, ag[0].v[3], ag[0].u[4], ag[1].start, ag[0].a[3], ag[0].v[4],
+        ag[1].u[1], ag[1].v[1], ag[1].start_a, ag[0].a[4], ag[1].u[2], ag[0].finish, (loop.turn_left[0], (1,
+        ag[1].v[2]), (6, ag[1].a[1])), do.sent_left[0], (loop.product[0], (2, ag[1].u[3]), (4, ag[1].v[3]), (5,
+        ag[1].a[2]), (7, ag[1].u[4])), ag[1].v[4], do.kept, (loop.turn_product[0], (3, ag[1].a[3])), rk[0].start,
+        ag[1].a[4], ag[1].finish, (loop.turn_left[1],), do.sent_left[1], rk[0].one, do.sent_product[0],
+        (loop.product[1], (5, rk[0].two)), rk[0].three, (loop.turn_product[1], (6, rk[0].four)), rk[1].start,
+        rk[0].five, rk[1].one, do.sent_product[1], rk[0].six, do.rows[0], gk[0].zero, rk[1].two, rk[1].three,
+        gk[0].two, rk[1].four, gk[0].one, rk[1].five, gk[0].four, gk[0].three, rk[1].six, do.rows[1], gk[1].zero,
+        gk[0].five, gk[0].six, gk[0].finish, (loop.turn_grad[0], (3, gk[1].one), (4, gk[1].two)),
+        (loop.left_product[0], (3, gk[1].three), (5, gk[1].four)), gk[1].five, (loop.turn_back[0], (7, gk[1].six)),
+        rj[0].start, gk[1].finish, (loop.turn_grad[1], (6, rj[0].a[1]), (7, rj[0].start_v), (7, rj[0].u[1])),
+        do.fetch_v, (loop.left_product[1], (3, rj[0].a[2]), (5, rj[0].v[1]), (6, rj[0].u[2])), do.fetch_s,
+        (loop.turn_back[1], (1, rj[0].a[3]), (7, rj[0].v[2])), rj[1].start, rj[0].u[3], (loop.right_product, (4,
+        rj[0].a[4]), (7, rj[1].start_v), (7, rj[0].v[3]), (9, rj[1].a[1]), (11, rj[1].u[1]), (14, rj[0].u[4])),
+        do.fetched, (loop.right_pull, (1, rj[1].v[1]), (1, rj[0].v[4]), (3, rj[1].a[2]), (3, do.save[0]), (4,
+        rj[1].u[2]), (6, rj[1].v[2]), (6, do.save[1]), (7, rj[1].a[3]), (7, rj[0].finish), (7, do.left_pull[0]), (7,
+        rj[1].u[3]), (9, rj[1].v[3]), (9, do.save[2]), (10, rj[1].a[4])), rj[1].u[4], do.save[3], rj[1].v[4],
+        rj[1].finish, do.left_pull[1],
     )
 
 
 def kernel(
     pair, slab, gain, left_gate, left_value, right_gate, right_value, out_gain, out_weight, cot,
-    update, grad_pair, grad_slab,
+    update, grad_pair, grad_slab, s_kept, v_kept,
     xv, wl_up, wl_low, wlc_hi, wlc_lo, wr_up, wr_low, wrc_hi, wrc_lo,
     W, Rt, Lt, Gt, Hb, N, Q, x1a, x1b, y2, x2a, x2b, y1, ry, first, rest, rf, ss, rs, local,
 ):
@@ -549,10 +557,31 @@
     Nf = N.reshape(C * 16 * NR, B, 128)
     flat_R = Rt.reshape(128 * B, 128)
     flat_H = Hb.reshape(128 * HS, 128)
+    flat_G = Gt.reshape(128 * 128, 128)
+    flat_N = N.reshape(C * 16 * NR * B, 128)
+    flat_W = W.reshape(C * 16 * NR * B, 128)
+    factors = pl.ds(0, B * B)
+    keep = [
+        pltpu.make_async_copy(flat_G.at[factors], s_kept, local.at[5]),
+        pltpu.make_async_copy(flat_N.at[factors], v_kept, local.at[6]),
+    ]
+    fetch = [
+        pltpu.make_async_copy(s_kept, flat_R.at[factors], local.at[7]),
+        pltpu.make_async_copy(v_kept, flat_W.at[factors], local.at[8]),
+    ]
+
+    def fetch_v():
+        net.drain(*[("gk", c) for c in range(C)])
+        fetch[1].start()
+
     K = 8
 
     def right(t):
-        made = forward(xv[pl.ds(t * K, K)].reshape(K * B, 128), wr_up, wr_low)
+        s, v = gates(normalise(xv[pl.ds(t * K, K)].reshape(K * B, 128))[0], wr_up, wr_low)
+        part = pl.ds(t * K * B, K * B)
+        flat_G[part, :] = s
+        flat_N[part, :] = v
+        made = s * v
         for u in range(K):
             tile = jnp.concatenate([made[u * B : (u + 1) * B], jnp.zeros((32, 128), f32)], 0).T
             flat_R[pl.ds(t * K + u, 128, stride=B), :] = tile
@@ -579,7 +608,8 @@
     def right_pull(t):
         grads = [flat_H[pl.ds(t * K + u, 128, stride=HS), :].T[:B] for u in range(K)]
         rows = xv[pl.ds(t * K, K)].reshape(K * B, 128)
-        out = pull(rows, jnp.concatenate(grads, 0), wr_up, wr_low, wrc_hi, wrc_lo)
+        part = pl.ds(t * K * B, K * B)
+        out = pull(rows, jnp.concatenate(grads, 0), flat_R[part, :], flat_W[part, :], wrc_hi, wrc_lo)
         xv[pl.ds(t * K, K)] = out.reshape(K, B, 128)
 
     def turn_in(dst, c):
@@ -625,7 +655,9 @@
     def left_pull(c):
         def step():
             grads = N[(c, net.yh) + net.zs[0]].reshape(NR * B, 128)
-            out = pull(slab[c * NR : (c + 1) * NR].reshape(NR * B, 128), grads, wl_up, wl_low, wlc_hi, wlc_lo)
+            mine = slab[c * NR : (c + 1) * NR].reshape(NR * B, 128)
+            s, v = gates(normalise(mine)[0], wl_up, wl_low)
+            out = pull(mine, grads, s, v, wlc_hi, wlc_lo)
             grad_slab[c * NR : (c + 1) * NR] = out.reshape(NR, B, 128)
 
         return step
@@ -639,6 +671,11 @@
         prepare_right=lambda: prepare(gain, right_gate, right_value, wr_up, wr_low, wrc_hi, wrc_lo),
         entered=entered,
         loaded=load.wait,
+        keep=lambda: [copy.start() for copy in keep],
+        kept=lambda: [copy.wait() for copy in keep],
+        fetch_s=fetch[0].start,
+        fetch_v=fetch_v,
+        fetched=lambda: [copy.wait() for copy in fetch],
         left=[left(c) for c in each],
         rows=[rows(c) for c in each],
         left_pull=[left_pull(c) for c in each],
@@ -658,17 +695,32 @@
         save(k).wait()
 
 
+def hand_over(update_in, pair_in, slab_in, update, pair, slab, held, into, out):
+    parts = [(update_in, update, pl.ds(0, 8))]
+    parts += [(pair_in.at[pl.ds(k, 12)], pair.at[pl.ds(k, 12)], pl.ds(8 + k, 12)) for k in range(0, B, 12)]
+    parts += [(slab_in, slab, pl.ds(8 + B, 8))]
+    loads = [pltpu.make_async_copy(a, held.at[p], into.at[k]) for k, (a, _, p) in enumerate(parts)]
+    saves = [pltpu.make_async_copy(held.at[p], b, out.at[k]) for k, (_, b, p) in enumerate(parts)]
+    for load in loads:
+        load.start()
+    for load, save in zip(loads, saves):
+        load.wait()
+        save.start()
+    for save in saves:
+        save.wait()
+
+
 def shards(
     pair_map, slab_rows, norm_gain, left_gate, left_value, right_gate, right_value, out_gain, out_weight, cotangent
 ):
     S = jax.ShapeDtypeStruct
     M = pltpu.VMEM
     weights = [M((256, 256), bf16)] + [M((128, 256), bf16)] * 3
-    return pl.pallas_call(
+    made = pl.pallas_call(
         kernel,
-        out_shape=[S((8,) + T, f32), S((B,) + T, f32), S((8,) + T, f32)],
+        out_shape=[S((8,) + T, f32), S((B,) + T, f32), S((8,) + T, f32)] + [S((B * B, 128), f32)] * 2,
         in_specs=[HBM] + [VM] * 9,
-        out_specs=[VM, HBM, VM],
+        out_specs=[VM, HBM, VM, HBM, HBM],
         scratch_shapes=[M((B,) + T, f32)]
         + weights * 2
         + [
@@ -691,14 +743,23 @@
             M((C, HR) + T, f32),
             pltpu.SemaphoreType.DMA((240,)),
             pltpu.SemaphoreType.DMA((240,)),
-            pltpu.SemaphoreType.DMA((5,)),
+            pltpu.SemaphoreType.DMA((9,)),
         ],
-        compiler_params=pltpu.CompilerParams(collective_id=1, has_side_effects=True, vmem_limit_bytes=63 * MIB),
+        compiler_params=pltpu.CompilerParams(collective_id=1, has_side_effects=True, vmem_limit_bytes=63 * MIB + MIB // 2),
         name="triangle",
     )(
         pair_map, slab_rows, norm_gain.reshape(1, 128), left_gate, left_value, right_gate, right_value,
         out_gain.reshape(1, 128), out_weight, cotangent,
     )
+    return pl.pallas_call(
+        hand_over,
+        out_shape=[S((8,) + T, f32), S((B,) + T, f32), S((8,) + T, f32)],
+        in_specs=[HBM] * 3,
+        out_specs=[HBM] * 3,
+        scratch_shapes=[M((B + 16,) + T, f32), pltpu.SemaphoreType.DMA((10,)), pltpu.SemaphoreType.DMA((10,))],
+        compiler_params=pltpu.CompilerParams(vmem_limit_bytes=16 * MIB),
+        name="hand_over",
+    )(*made[:3])
 
 
 def solution(mesh):

time: 182 us -> 180 us (0.989)
  local copies, waits for them, and re-layouts: 7.41 us -> 4.32 us
  Pallas kernels: 172 us -> 174 us
    pallas_call x0 -> x1, Pallas kernels: none -> 3.91 us  [shards(): pl.pallas_call(hand_over, out_shape=[S((8,) + T, f32), S((B,) + T, f32),...]
    unnamed x5 -> x6, local copies, waits for them, and re-layouts: 7.41 us -> 4.32 us
where the time goes in v4:
time: 180 us; the launch traced here: 179 us
  Pallas kernels  174 us (97%)
  local copies, waits for them, and re-layouts  4.32 us (2%)
    pallas_call x1, Pallas kernels, shards(): pl.pallas_call(kernel, out_shape=[S((8,) + T, f32), S((B,) + T, f32), S((...  170 us
    unnamed x6, local copies, waits for them, and re-layouts  4.32 us
    pallas_call x1, Pallas kernels, shards(): pl.pallas_call(hand_over, out_shape=[S((8,) + T, f32), S((B,) + T, f32),...  3.91 us

profile of v4, /device:TPU:2, one launch (start us, length us, event | category | flops | bytes accessed | tf_op | source)
XLA Modules:
  0.0 179.0 jit_solution(3559349052323991020)
XLA Ops:
  0.6 170.2 %triangle.1 = (f32[8,96,128]{2,1,0:T(8,128)}, f32[96,96,128]{2,1,0:T(8,128)}, f32[8,96,128]{2,1,0:T(8,128)}, f32[9216,128]{1,0:T(8,128)}, f32[9216,128]{1,0:T(8,128)}) custom-call(f32[96,96,128]{2,1,0:T(8,128)} %pair.1, f32[8,96,128]{2,1,0:T(8,128)} %slab.1, f32[1,128]{1,0:T(1,128)} %bitcast.2, f32[128,128]{1,0:T(8,128)} %left_gate.1, ...), custom_call_target="tpu_custom_call" | custom-call | tf_op jit(solution)/shard_map/triangle/pallas_call | solution.py:719
  170.8 0.0 copy-start
  170.8 2.3 %copy-done = f32[96,96,128]{2,1,0:T(8,128)S(1)} copy-done((f32[96,96,128]{2,1,0:T(8,128)S(1)}, f32[96,96,128]{2,1,0:T(8,128)}, u32[]{:S(2)}) %copy-start) | copy-done | bytes 4718616
  173.1 0.0 copy-start.1
  173.1 1.0 copy-done.1
  174.1 0.0 copy-start.2
  174.1 1.0 copy-done.2
  175.1 3.9 %hand_over.1 = (f32[8,96,128]{2,1,0:T(8,128)}, f32[96,96,128]{2,1,0:T(8,128)}, f32[8,96,128]{2,1,0:T(8,128)}) custom-call(f32[8,96,128]{2,1,0:T(8,128)S(1)} %copy-done.1, f32[96,96,128]{2,1,0:T(8,128)S(1)} %copy-done, f32[8,96,128]{2,1,0:T(8,128)S(1)} %copy-done.2), custom_call_target="tpu_custom_call" | custom-call | tf_op jit(solution)/shard_map/hand_over/pallas_call | solution.py:754
Async XLA Ops:
  170.8 2.3 %copy-start = (f32[96,96,128]{2,1,0:T(8,128)S(1)}, f32[96,96,128]{2,1,0:T(8,128)}, u32[]{:S(2)}) copy-start(f32[96,96,128]{2,1,0:T(8,128)} %get-tuple-element.7.pair_in) | copy-start | bytes 14155780
  173.1 1.0 copy-start.1
  174.1 1.0 copy-start.2

commit v5 on v4

--- a/solution.py
+++ b/solution.py
@@ -514,25 +514,24 @@
 def order(ag, rk, gk, rj, do, loop):
     return (
         do.prepare_left, do.left[0], do.entered, ag[0].start, do.left[1], do.prepare_right, do.loaded, (loop.right,
-        (2, ag[0].u[1]), (2, ag[0].start_a), (3, ag[0].v[1]), (5, ag[0].u[2]), (7, ag[0].a[1]), (9, ag[0].v[2]),
-        (10, ag[0].u[3])), ag[0].a[2], do.keep, ag[0].v[3], ag[0].u[4], ag[1].start, ag[0].a[3], ag[0].v[4],
-        ag[1].u[1], ag[1].v[1], ag[1].start_a, ag[0].a[4], ag[1].u[2], ag[0].finish, (loop.turn_left[0], (1,
-        ag[1].v[2]), (6, ag[1].a[1])), do.sent_left[0], (loop.product[0], (2, ag[1].u[3]), (4, ag[1].v[3]), (5,
-        ag[1].a[2]), (7, ag[1].u[4])), ag[1].v[4], do.kept, (loop.turn_product[0], (3, ag[1].a[3])), rk[0].start,
-        ag[1].a[4], ag[1].finish, (loop.turn_left[1],), do.sent_left[1], rk[0].one, do.sent_product[0],
-        (loop.product[1], (5, rk[0].two)), rk[0].three, (loop.turn_product[1], (6, rk[0].four)), rk[1].start,
-        rk[0].five, rk[1].one, do.sent_product[1], rk[0].six, do.rows[0], gk[0].zero, rk[1].two, rk[1].three,
-        gk[0].two, rk[1].four, gk[0].one, rk[1].five, gk[0].four, gk[0].three, rk[1].six, do.rows[1], gk[1].zero,
-        gk[0].five, gk[0].six, gk[0].finish, (loop.turn_grad[0], (3, gk[1].one), (4, gk[1].two)),
-        (loop.left_product[0], (3, gk[1].three), (5, gk[1].four)), gk[1].five, (loop.turn_back[0], (7, gk[1].six)),
-        rj[0].start, gk[1].finish, (loop.turn_grad[1], (6, rj[0].a[1]), (7, rj[0].start_v), (7, rj[0].u[1])),
-        do.fetch_v, (loop.left_product[1], (3, rj[0].a[2]), (5, rj[0].v[1]), (6, rj[0].u[2])), do.fetch_s,
-        (loop.turn_back[1], (1, rj[0].a[3]), (7, rj[0].v[2])), rj[1].start, rj[0].u[3], (loop.right_product, (4,
-        rj[0].a[4]), (7, rj[1].start_v), (7, rj[0].v[3]), (9, rj[1].a[1]), (11, rj[1].u[1]), (14, rj[0].u[4])),
-        do.fetched, (loop.right_pull, (1, rj[1].v[1]), (1, rj[0].v[4]), (3, rj[1].a[2]), (3, do.save[0]), (4,
-        rj[1].u[2]), (6, rj[1].v[2]), (6, do.save[1]), (7, rj[1].a[3]), (7, rj[0].finish), (7, do.left_pull[0]), (7,
-        rj[1].u[3]), (9, rj[1].v[3]), (9, do.save[2]), (10, rj[1].a[4])), rj[1].u[4], do.save[3], rj[1].v[4],
-        rj[1].finish, do.left_pull[1],
+        (3, ag[0].u[1]), (3, ag[0].start_a), (5, ag[0].v[1]), (7, ag[0].u[2]), (9, ag[0].a[1]), (11, ag[0].v[2])),
+        do.keep, ag[0].u[3], ag[0].a[2], ag[0].v[3], ag[0].u[4], ag[1].start, ag[0].a[3], ag[0].v[4], ag[1].u[1],
+        ag[1].v[1], ag[1].start_a, ag[0].a[4], ag[1].u[2], ag[1].v[2], ag[0].finish, (loop.turn_left[0], (5,
+        ag[1].a[1])), do.sent_left[0], (loop.product[0], (1, ag[1].u[3]), (4, ag[1].v[3]), (6, ag[1].a[2]), (7,
+        ag[1].u[4])), do.kept, (loop.turn_product[0], (1, ag[1].v[4])), rk[0].start, ag[1].a[3], ag[1].a[4],
+        ag[1].finish, rk[0].one, do.sent_product[0], (loop.turn_left[1],), do.sent_left[1], (loop.product[1], (3,
+        rk[0].two), (7, rk[0].three)), (loop.turn_product[1], (5, rk[0].four)), rk[1].start, rk[0].five, rk[1].one,
+        do.sent_product[1], rk[0].six, do.rows[0], gk[0].zero, rk[1].two, rk[1].three, gk[0].two, rk[1].four,
+        gk[0].one, rk[1].five, gk[0].four, gk[0].three, rk[1].six, do.rows[1], gk[1].zero, gk[0].five, gk[0].six,
+        gk[0].finish, (loop.turn_grad[0], (5, gk[1].one), (7, gk[1].two)), (loop.left_product[0], (5, gk[1].three)),
+        gk[1].four, (loop.turn_back[0], (7, gk[1].five)), rj[0].start, gk[1].six, rj[0].a[1], gk[1].finish,
+        rj[0].start_v, rj[0].u[1], (loop.turn_grad[1],), do.fetch_v, (loop.left_product[1], (1, rj[0].a[2]), (3,
+        rj[0].v[1]), (5, rj[0].u[2])), rj[0].a[3], do.fetch_s, (loop.turn_back[1], (5, rj[0].v[2])), rj[1].start,
+        rj[0].u[3], (loop.right_product, (4, rj[0].a[4]), (8, rj[0].v[3]), (8, rj[1].start_v), (10, rj[1].a[1]),
+        (12, rj[1].u[1]), (15, rj[0].u[4])), do.fetched, (loop.right_pull, (2, rj[0].v[4]), (3, rj[1].v[1]), (3,
+        do.save[0]), (4, rj[1].a[2]), (6, rj[1].u[2]), (6, do.save[1]), (7, rj[1].v[2]), (9, rj[1].a[3]), (9,
+        do.save[2]), (10, rj[0].finish), (10, rj[1].u[3]), (10, do.left_pull[0]), (11, rj[1].v[3])), rj[1].a[4],
+        do.save[3], rj[1].u[4], rj[1].v[4], rj[1].finish, do.left_pull[1],
     )
 
 
@@ -757,7 +756,7 @@
         in_specs=[HBM] * 3,
         out_specs=[HBM] * 3,
         scratch_shapes=[M((B + 16,) + T, f32), pltpu.SemaphoreType.DMA((10,)), pltpu.SemaphoreType.DMA((10,))],
-        compiler_params=pltpu.CompilerParams(vmem_limit_bytes=16 * MIB),
+        compiler_params=pltpu.CompilerParams(vmem_limit_bytes=62 * MIB),
         name="hand_over",
     )(*made[:3])
 

time: 180 us -> 171 us (0.950)
  local copies, waits for them, and re-layouts: 4.32 us -> 0 us
  Pallas kernels: 174 us -> 170 us
    pallas_call x1, Pallas kernels: 170 us -> 165 us  [shards(): pl.pallas_call(kernel, out_shape=[S((8,) + T, f32), S((B,) + T, f32), S((...]
    unnamed x6 -> x0, local copies, waits for them, and re-layouts: 4.32 us -> none
where the time goes in v5:
time: 171 us; the launch traced here: 170 us
  Pallas kernels  170 us (99%)
    pallas_call x1, Pallas kernels, shards(): pl.pallas_call(kernel, out_shape=[S((8,) + T, f32), S((B,) + T, f32), S((...  165 us
    pallas_call x1, Pallas kernels, shards(): pl.pallas_call(hand_over, out_shape=[S((8,) + T, f32), S((B,) + T, f32),...  4.88 us

profile of v5, /device:TPU:2, one launch (start us, length us, event | category | flops | bytes accessed | tf_op | source)
XLA Modules:
  0.0 170.2 jit_solution(12910884750906277403)
XLA Ops:
  0.6 164.7 %triangle.1 = (f32[8,96,128]{2,1,0:T(8,128)}, f32[96,96,128]{2,1,0:T(8,128)}, f32[8,96,128]{2,1,0:T(8,128)}, f32[9216,128]{1,0:T(8,128)}, f32[9216,128]{1,0:T(8,128)}) custom-call(f32[96,96,128]{2,1,0:T(8,128)} %pair.1, f32[8,96,128]{2,1,0:T(8,128)} %slab.1, f32[1,128]{1,0:T(1,128)} %bitcast.2, f32[128,128]{1,0:T(8,128)} %left_gate.1, ...), custom_call_target="tpu_custom_call" | custom-call | tf_op jit(solution)/shard_map/triangle/pallas_call | solution.py:718
  165.4 4.9 %hand_over.1 = (f32[8,96,128]{2,1,0:T(8,128)}, f32[96,96,128]{2,1,0:T(8,128)}, f32[8,96,128]{2,1,0:T(8,128)}) custom-call(f32[8,96,128]{2,1,0:T(8,128)} %get-tuple-element.6.update_in, f32[96,96,128]{2,1,0:T(8,128)} %get-tuple-element.7.pair_in, f32[8,96,128]{2,1,0:T(8,128)} %get-tuple-element.8.slab_in), custom_call_target="tpu_custom_call" | custom-call | tf_op jit(solution)/shard_map/hand_over/pallas_call | solution.py:753
